TPU v7x, 256 devices: a whole 4x4x8 slice. The times are simulated.
256 devices in a mesh: ctx: 64 (over z_lo, y, x), head: 4 (over z_hi, core).
Axes of the slice: x: 4, y: 4, z: 8 (z_hi: 2, z_lo: 4; z = z_hi * 4 + z_lo), core: 2. Of those that a mesh axis runs over, the one named last changes fastest.
Arguments:
- queries: bfloat16 [16384, 8192], P(('ctx', 'head')), may hold values from -9 to 9
- keys: bfloat16 [16384, 512], P('ctx', 'head'), may hold values from -9 to 9
- values: bfloat16 [16384, 512], P('ctx', 'head'), may hold values from -6 to 6
- doc_lengths: int32 [8], replicated, may hold values from 1 to 8192, 16384 in all
Outputs:
- attended: bfloat16 [16384, 8192], P(('ctx', 'head'))
Inputs may be any that keep to these rules, and one draw needn't show every extreme that they name: `doc_lengths`: the lengths sum to 16384 and the largest is exactly 8192.
All inputs are finite; a program needn't handle non-finite values.
Results may differ from a plain program's by a relative error of at most 0.0055.
Values may be sent and summed in bfloat16 or wider, within the bound.
A program may use at most 64 MiB of HBM per device.

v0:
```python
import math

import jax
import jax.numpy as jnp
from jax import lax
from jax.sharding import PartitionSpec as P

neg_big = -1e30
block_keys = 512


def token_begins(doc_starts, positions):
    hit = doc_starts[None, :] <= positions[:, None]
    return jnp.max(jnp.where(hit, doc_starts[None, :], 0), axis=1)


def absorb(
    carried, held_tiles, tile_starts, doc_starts, key_piece, value_piece, piece_start, tok_rows
):
    top_scores, denominators, runnings = carried
    piece_rows = key_piece.shape[0]
    block_width = math.gcd(piece_rows, block_keys)
    tile_count, query_rows, head_depth = held_tiles.shape
    group_size = query_rows // tok_rows
    score_scale = 1.0 / math.sqrt(head_depth)
    new_tops, new_denoms, new_runs = ([], [], [])
    for tile_num in range(tile_count):
        tile_start = tile_starts[tile_num]
        positions = tile_start + jnp.arange(tok_rows, dtype=jnp.int32)
        begins = token_begins(doc_starts, positions)
        low_pos = jnp.maximum(begins[0], piece_start)
        high_pos = jnp.minimum(tile_start + tok_rows, piece_start + piece_rows)
        first_block = low_pos // block_width
        last_block = jnp.maximum(first_block, (high_pos + block_width - 1) // block_width)
        tile_query = held_tiles[tile_num]

        def add_block(block_index, loop_state):
            top_score, denominator, running = loop_state
            offset = block_index * block_width
            key_block = lax.dynamic_slice_in_dim(key_piece, offset, block_width, 0)
            value_block = lax.dynamic_slice_in_dim(value_piece, offset, block_width, 0)
            scores = (
                lax.dot_general(
                    tile_query,
                    key_block,
                    (((1,), (1,)), ((), ())),
                    preferred_element_type=jnp.float32,
                )
                * score_scale
            )
            key_pos = offset + jnp.arange(block_width, dtype=jnp.int32)
            visible = (key_pos[None, :] <= positions[:, None]) & (
                key_pos[None, :] >= begins[:, None]
            )
            visible = jnp.repeat(visible, group_size, axis=0)
            new_top = jnp.maximum(top_score, jnp.max(jnp.where(visible, scores, neg_big), axis=1))
            weights = jnp.where(visible, jnp.exp(scores - new_top[:, None]), 0.0)
            rescale = jnp.exp(top_score - new_top)
            denominator = denominator * rescale + jnp.sum(weights, axis=1)
            running = running * rescale[:, None] + jnp.dot(
                weights.astype(jnp.bfloat16), value_block, preferred_element_type=jnp.float32
            )
            return (new_top, denominator, running)

        result = lax.fori_loop(
            first_block,
            last_block,
            add_block,
            (top_scores[tile_num], denominators[tile_num], runnings[tile_num]),
        )
        new_tops.append(result[0])
        new_denoms.append(result[1])
        new_runs.append(result[2])
    return (jnp.stack(new_tops), jnp.stack(new_denoms), jnp.stack(new_runs))


def per_device(queries, keys, values, doc_lengths):
    by_head = lax.all_to_all(queries, "head", split_axis=1, concat_axis=0, tiled=True)
    tok_dev = by_head.shape[0]
    head_depth = keys.shape[1]
    group_size = by_head.shape[1] // head_depth
    tile_count = 8
    tok_rows = tok_dev // tile_count
    shard_index = lax.axis_index("ctx")
    doc_starts = jnp.cumsum(doc_lengths) - doc_lengths
    tile_query = by_head.reshape(tile_count, tok_rows * group_size, head_depth)
    tile_starts = shard_index * tok_dev + jnp.arange(tile_count, dtype=jnp.int32) * tok_rows
    query_rows = tok_rows * group_size
    initial = (
        jnp.full((tile_count, query_rows), neg_big, jnp.float32),
        jnp.zeros((tile_count, query_rows), jnp.float32),
        jnp.zeros((tile_count, query_rows, head_depth), jnp.float32),
    )
    whole_keys, whole_values = (
        lax.all_gather(keys, "ctx", axis=0, tiled=True),
        lax.all_gather(values, "ctx", axis=0, tiled=True),
    )
    carried = absorb(
        initial,
        tile_query,
        tile_starts,
        doc_starts,
        whole_keys,
        whole_values,
        jnp.int32(0),
        tok_rows,
    )
    results = (carried[2] / carried[1][..., None]).astype(jnp.bfloat16)
    merged = results.reshape(tok_dev, group_size * head_depth)
    return lax.all_to_all(merged, "head", split_axis=0, concat_axis=1, tiled=True)


def solution(mesh):
    in_specs = (P(("ctx", "head"), None), P("ctx", "head"), P("ctx", "head"), P())
    out_specs = P(("ctx", "head"), None)
    return jax.shard_map(
        per_device, mesh=mesh, in_specs=in_specs, out_specs=out_specs, check_vma=False
    )
```

profile of v0, /device:TPU:60, one launch (start us, length us, event | category | flops | bytes accessed | tf_op | source)
XLA Modules:
  0.0 1235.2 jit_solution(8198677841830438668)
XLA Ops:
  8.0 2.3 copy.81
  10.3 7.6 all-to-all-start
  29.0 18.4 %all-to-all-done = bf16[64,4,2048]{2,0,1:T(8,128)(2,1)S(1)} async-done(((bf16[64,4,2048]{2,0,1:T(8,128)(2,1)}), bf16[64,4,2048]{2,0,1:T(8,128)(2,1)S(1)}, u32[]{:S(2)}, u32[]{:S(2)}) %all-to-all-start) | async-done | bytes 1048608 | tf_op jit(solution)/shard_map/all_to_all | solution.py:78
  48.0 273.4 %all-gather.3.cloned.1.call-done = bf16[16384,128]{1,0:T(8,128)(2,1)} async-done(((bf16[256,128]{1,0:T(8,128)(2,1)}), bf16[16384,128]{1,0:T(8,128)(2,1)}) %all-gather.3.cloned.1.call-update) | async-done | bytes 4194320 | tf_op jit(solution)/shard_map/all_gather | solution.py:95
  321.4 348.8 %all-gather.5.cloned.1.call-done = bf16[16384,128]{1,0:T(8,128)(2,1)} async-done(((bf16[256,128]{1,0:T(8,128)(2,1)}), bf16[16384,128]{1,0:T(8,128)(2,1)}) %all-gather.5.cloned.1.call-update) | async-done | bytes 4194320 | tf_op jit(solution)/shard_map/all_gather | solution.py:96
  670.3 65.5 %while.121 = (s32[]{:T(128)}, f32[512]{0:T(512)S(1)}, f32[512]{0:T(512)S(1)}, f32[512,128]{1,0:T(8,128)S(1)}, s32[]{:T(128)}, /*index=5*/s32[32]{0:T(128)S(1)}, ...) while((s32[]{:T(128)}, f32[512]{0:T(512)S(1)}, ...), condition=%wide.region_10.11_spmd.clone, body=%wide.region_7.10_spmd.clone.sunk | while | flops 136758816 | bytes 5706307 | solution.py:65
  677.0 1.4 convolution_add_fusion.17
  735.8 66.4 %while.122 = (s32[]{:T(128)}, f32[512]{0:T(512)S(1)}, f32[512]{0:T(512)S(1)}, f32[512,128]{1,0:T(8,128)S(1)}, s32[]{:T(128)}, /*index=5*/s32[32]{0:T(128)S(1)}, ...) while((s32[]{:T(128)}, f32[512]{0:T(512)S(1)}, ...), condition=%wide.region_15.16_spmd.clone, body=%wide.region_12.15_spmd.clone.sunk | while | flops 136758816 | bytes 5706307 | solution.py:65
  742.7 1.4 convolution_add_fusion.18
  751.0 1.4 convolution_add_fusion.18
  759.3 1.4 convolution_add_fusion.18
  802.3 66.5 %while.123 = (s32[]{:T(128)}, f32[512]{0:T(512)S(1)}, f32[512]{0:T(512)S(1)}, f32[512,128]{1,0:T(8,128)S(1)}, s32[]{:T(128)}, /*index=5*/s32[32]{0:T(128)S(1)}, ...) while((s32[]{:T(128)}, f32[512]{0:T(512)S(1)}, ...), condition=%wide.region_20.21_spmd.clone, body=%wide.region_17.20_spmd.clone.sunk | while | flops 136758816 | bytes 5706307 | solution.py:65
  813.3 1.4 convolution_add_fusion.19
  825.8 1.4 convolution_add_fusion.19
  838.3 1.4 convolution_add_fusion.19
  850.8 1.4 convolution_add_fusion.19
  863.2 1.4 convolution_add_fusion.19
  868.9 65.3 %while.124 = (s32[]{:T(128)}, f32[512]{0:T(512)S(1)}, f32[512]{0:T(512)S(1)}, f32[512,128]{1,0:T(8,128)S(1)}, s32[]{:T(128)}, /*index=5*/s32[32]{0:T(128)S(1)}, ...) while((s32[]{:T(128)}, f32[512]{0:T(512)S(1)}, ...), condition=%wide.region_25.26_spmd.clone, body=%wide.region_22.25_spmd.clone.sunk | while | flops 136758816 | bytes 5706307 | solution.py:65
  934.2 66.5 %while.125 = (s32[]{:T(128)}, f32[512]{0:T(512)S(1)}, f32[512]{0:T(512)S(1)}, f32[512,128]{1,0:T(8,128)S(1)}, s32[]{:T(128)}, /*index=5*/s32[32]{0:T(128)S(1)}, ...) while((s32[]{:T(128)}, f32[512]{0:T(512)S(1)}, ...), condition=%wide.region_30.31_spmd.clone, body=%wide.region_27.30_spmd.clone.sunk | while | flops 136758816 | bytes 5706307 | solution.py:65
  1000.8 65.8 %while.126 = (s32[]{:T(128)}, f32[512]{0:T(512)S(1)}, f32[512]{0:T(512)S(1)}, f32[512,128]{1,0:T(8,128)S(1)}, s32[]{:T(128)}, /*index=5*/s32[32]{0:T(128)S(1)}, ...) while((s32[]{:T(128)}, f32[512]{0:T(512)S(1)}, ...), condition=%wide.region_35.36_spmd.clone, body=%wide.region_32.35_spmd.clone.sunk | while | flops 136758816 | bytes 5706307 | solution.py:65
  1066.6 66.7 %while.127 = (s32[]{:T(128)}, f32[512]{0:T(512)S(1)}, f32[512]{0:T(512)S(1)}, f32[512,128]{1,0:T(8,128)S(1)}, s32[]{:T(128)}, /*index=5*/s32[32]{0:T(128)S(1)}, ...) while((s32[]{:T(128)}, f32[512]{0:T(512)S(1)}, ...), condition=%wide.region_40.41_spmd.clone, body=%wide.region_37.40_spmd.clone.sunk | while | flops 136758816 | bytes 5706307 | solution.py:65
  1133.4 65.6 %while.120 = (s32[]{:T(128)}, f32[512]{0:T(512)S(1)}, f32[512]{0:T(512)S(1)}, f32[512,128]{1,0:T(8,128)S(1)}, s32[]{:T(128)}, /*index=5*/s32[32]{0:T(128)S(1)}, ...) while((s32[]{:T(128)}, f32[512]{0:T(512)S(1)}, ...), condition=%wide.region_5.6_spmd.clone, body=%wide.region_2.5_spmd.clone.sunk | while | flops 136758816 | bytes 5706307 | solution.py:65
  1200.6 2.0 divide_convert_fusion
  1203.1 24.2 %all_to_all.32 = bf16[4,64,2048]{2,1,0:T(8,128)(2,1)S(1)} all-to-all(bf16[4,64,2048]{2,1,0:T(8,128)(2,1)S(1)} %convert_element_type.33), channel_id=1, replica_groups=mesh['ctx'=64,'head'=4] {'head'}, dimensions={0} | all-to-all | bytes 2097152 | tf_op jit(solution)/shard_map/all_to_all | solution.py:110
  (1453 shorter events, 515.3 us)
Async XLA Ops:
  6.5 12.6 %copy-start.1 = (s32[8]{0:T(128)S(1)}, s32[8]{0:T(128)}, u32[]{:S(2)}) copy-start(s32[8]{0:T(128)} %param.23) | copy-start | bytes 100
  6.5 314.9 %all-gather.3.cloned.1.call-start = ((), (), s32[]{:S(2)}) async-start(), calls=%async_computation.2 | async-start | bytes 4259840 | tf_op jit(solution)/shard_map/all_gather | solution.py:95
  7.3 663.0 %all-gather.5.cloned.1.call-start = ((), (), s32[]{:S(2)}) async-start(), calls=%async_computation.3 | async-start | bytes 4259840 | tf_op jit(solution)/shard_map/all_gather | solution.py:96
  10.3 37.1 %all-to-all-start = ((bf16[64,4,2048]{2,0,1:T(8,128)(2,1)}), bf16[64,4,2048]{2,0,1:T(8,128)(2,1)S(1)}, u32[]{:S(2)}, u32[]{:S(2)}) async-start(bf16[64,4,2048]{2,0,1:T(8,128)(2,1)} %bitcast.106), calls=%async_computation | async-start | bytes 2097152 | tf_op jit(solution)/shard_map/all_to_all | solution.py:78
  1199.3 1.4 copy-start
Sparse Core Ops, SparseCore 0:
  9.1 312.2 all-gather.2
  323.2 346.9 all-gather.4
where the time goes:
time: 1240 us
  waiting for transfers between devices  642 us (52%)
  matrix products  340 us (27%)
  other arithmetic  130 us (10%)
  local copies, waits for them, and re-layouts  60.4 us (5%)
  blocking collectives  24.2 us (2%)
  between operations  19.2 us (2%)
    all_gather x1, waiting for transfers between devices, per_device(): lax.all_gather(values, 'ctx', axis=0, tiled=True)  349 us
    all_gather x1, waiting for transfers between devices, per_device(): lax.all_gather(keys, 'ctx', axis=0, tiled=True)  273 us
    dot_general x128, matrix products, add_block(): jnp.dot(weights.astype(jnp.bfloat16), value_block, preferred_element_type...  181 us
    dot_general x128, matrix products, add_block(): lax.dot_general(tile_query, key_block, (((1,), (1,)), ((), ())), preferre...  159 us
    add x132, other arithmetic, absorb(): positions = tile_start + jnp.arange(tok_rows, dtype=jnp.int32)  80.7 us
    reshape x128, local copies, waits for them, and re-layouts, add_block(): visible = jnp.repeat(visible, group_size, axis=0)  44 us
    reduce_sum x128, other arithmetic, add_block(): denominator = denominator * rescale + jnp.sum(weights, axis=1)  34 us
  transfers between devices with their start and end apart: 3, of which 3 were waited for; matrix products, arithmetic and copies ran while one was open for 1% of the time, Pallas kernels for 0%

commit v1 on v0

--- a/solution.py
+++ b/solution.py
@@ -3,12 +3,448 @@
 import jax
 import jax.numpy as jnp
 from jax import lax
+from jax.experimental import pallas as pl
+from jax.experimental.pallas import tpu as pltpu
 from jax.sharding import PartitionSpec as P
 
 neg_big = -1e30
 block_keys = 512
-
-
+MESH = pl.DeviceIdType.MESH
+
+head_depth = 128
+heads_per_group = 16
+group_columns = heads_per_group * head_depth
+own_tokens = 64
+block = 256
+row_keys = 4 * block
+slot_columns = own_tokens * heads_per_group
+exponent_scale = math.log2(math.e) / math.sqrt(head_depth)
+safe_exponent = 100.0
+
+
+def attend_kernel(
+    q_ref,
+    k_ref,
+    v_ref,
+    len_ref,
+    out_ref,
+    stat_ref,
+    stage,
+    keyval,
+    q_in,
+    q_cols,
+    acc,
+    denom,
+    begins,
+    o_part,
+    stat_own,
+    stat_in,
+    stage_sem,
+    row_sem,
+    q_sem,
+    o_sem,
+    stat_sem,
+    z_send,
+    plane_send,
+    q_send,
+    sib_send,
+    o_send,
+    stat_send,
+):
+    ctx = lax.axis_index("ctx")
+    head = lax.axis_index("head")
+    plane, y, x = ctx // 16, (ctx // 4) % 4, ctx % 4
+    half, core = head // 2, head % 2
+    ybit, xbit, yhi = y % 2, x % 2, y // 2
+    group = ybit * 2 + xbit
+    quad_row = plane * 4 + yhi * 2
+    receiver = core == xbit
+
+    def ctx_of(p, yy, xx):
+        return p * 16 + yy * 4 + xx
+
+    barrier = pltpu.get_barrier_semaphore()
+    partners = []
+    for dy in range(4):
+        for dx in range(4):
+            if dy or dx:
+                partners.append((ctx_of(plane, (y + dy) % 4, (x + dx) % 4), head))
+    for dz in range(1, 8):
+        z = (half * 4 + plane + dz) % 8
+        partners.append((ctx_of(z % 4, y, x), (z // 4) * 2 + core))
+    sibling = (ctx, half * 2 + 1 - core)
+    partners.append(sibling)
+    for partner in partners:
+        pl.semaphore_signal(barrier, inc=1, device_id=partner, device_id_type=MESH)
+
+    mine = half * 4 + plane
+    stage[mine, 0] = k_ref[...]
+    v_t = v_ref[...].T
+    stage[mine, 1] = jnp.concatenate([v_t[:, :128], v_t[:, 128:]], axis=0)
+    pl.semaphore_wait(barrier, len(partners))
+
+    def remote(src, dst, send, recv, target):
+        return pltpu.make_async_remote_copy(
+            src_ref=src,
+            dst_ref=dst,
+            send_sem=send,
+            recv_sem=recv,
+            device_id=target,
+            device_id_type=MESH,
+        )
+
+    def z_copy(n, flip, ahead):
+        to_half = (half + flip) % 2
+        return remote(
+            stage.at[mine],
+            stage.at[mine],
+            z_send.at[n],
+            stage_sem.at[mine],
+            (ctx_of(plane + ahead, y, x), to_half * 2 + core),
+        )
+
+    z_plan = [(1, 0), (0, 1), (1, 1), (0, 2), (1, 2)]
+    for n, (flip, ahead) in enumerate(z_plan):
+        pl.when(plane + ahead < 4)(lambda n=n, f=flip, a=ahead: z_copy(n, f, a).start())
+
+    def plane_copies(flip, back, act):
+        g = (half + flip) % 2
+        p = plane - back
+        index = g * 4 + p
+        n = flip * 3 + back
+        for to_yhi in range(2):
+            for to_xhi in range(2):
+                to_y, to_x = to_yhi * 2 + g, to_xhi * 2 + core
+                wanted = p >= 0
+                if back == 0:
+                    wanted &= yhi <= to_yhi
+                if back == 2:
+                    wanted &= yhi >= to_yhi
+                here = (to_y == y) & (to_x == x)
+                row = p * 4 + y
+                sem = plane_send.at[n * 4 + to_yhi * 2 + to_xhi]
+
+                @pl.when(wanted & jnp.logical_not(here))
+                def _():
+                    copy = remote(
+                        stage.at[index],
+                        keyval.at[row, :, x],
+                        sem,
+                        row_sem.at[row],
+                        (ctx_of(plane, to_y, to_x), head),
+                    )
+                    copy.start() if act == "start" else copy.wait_send()
+
+                if act == "start":
+
+                    @pl.when(wanted & here)
+                    def _():
+                        pltpu.make_async_copy(
+                            stage.at[index], keyval.at[row, :, x], row_sem.at[row]
+                        ).start()
+
+    def mate(k):
+        my, mx = (ybit + k // 2) % 2, (xbit + k % 2) % 2
+        return my, mx
+
+    def q_copy(k):
+        my, mx = mate(k)
+        columns = pl.ds(pl.multiple_of((my * 2 + mx) * group_columns, 128), group_columns)
+        return remote(
+            q_ref.at[:, columns],
+            q_in.at[group],
+            q_send.at[k],
+            q_sem.at[group],
+            (ctx_of(plane, yhi * 2 + my, (x // 2) * 2 + mx), head),
+        )
+
+    def slot_copy(k):
+        my, mx = mate(k)
+        slot = my * 2 + mx
+        return remote(q_in.at[slot], q_in.at[slot], q_send.at[0], q_sem.at[slot], sibling)
+
+    plane_copies(0, 0, "start")
+    for k in (1, 2, 3):
+        q_copy(k).start()
+
+    def relay(flip, back):
+        @pl.when(plane >= back)
+        def _():
+            index = ((half + flip) % 2) * 4 + plane - back
+            remote(
+                stage.at[index], stage.at[index], z_send.at[5], stage_sem.at[index], sibling
+            ).wait_recv()
+
+        plane_copies(flip, back, "start")
+
+    lane = lax.broadcasted_iota(jnp.int32, (8, 128), 1) % own_tokens
+    starts = []
+    total = jnp.int32(0)
+    for d in range(8):
+        starts.append(total)
+        total = total + len_ref[d]
+
+    def slot_position(slot):
+        c = ctx_of(plane, yhi * 2 + slot // 2, (x // 2) * 2 + slot % 2)
+        return c * block + head * own_tokens
+
+    for slot in range(4):
+        position = slot_position(slot) + lane
+        begin = jnp.zeros((8, 128), jnp.int32)
+        for start in starts:
+            begin = jnp.maximum(begin, jnp.where(position >= start, start, 0))
+        begins[slot] = begin
+
+    acc[...] = jnp.zeros_like(acc)
+    denom[...] = jnp.zeros_like(denom)
+    own_keys = k_ref[...].astype(jnp.float32)
+    key_norm = jnp.max(jnp.sum(own_keys * own_keys, axis=1))
+
+    def columns_of(slot, read):
+        best = jnp.zeros((1, 128), jnp.float32)
+        for pair in range(8):
+            two = read(pair)
+            tile = jnp.concatenate([two[:, :128], two[:, 128:]], axis=0)
+            turned = tile.astype(jnp.float32).T
+            best = jnp.maximum(best, jnp.sum(turned * turned, axis=0, keepdims=True))
+            at = pl.multiple_of(slot * slot_columns + pair * 128, 128)
+            q_cols[:, pl.ds(at, 128)] = turned.astype(jnp.bfloat16)
+        return best
+
+    def read_own(pair):
+        at = pl.multiple_of(group * group_columns + pair * 256, 128)
+        return q_ref[:, pl.ds(at, 256)]
+
+    query_norm = columns_of(group, read_own)
+
+    relay(1, 0)
+    relay(0, 1)
+    relay(1, 1)
+
+    for k in (1, 2, 3):
+        slot_copy(k).wait_recv()
+        my, mx = mate(k)
+        slot = my * 2 + mx
+        query_norm = jnp.maximum(
+            query_norm,
+            columns_of(slot, lambda pair, s=slot: q_in[s, :, pl.ds(pair * 256, 256)]),
+        )
+
+    rank = lax.broadcasted_iota(jnp.int32, (8, 128), 0)
+    stat_own[0] = jnp.where(rank < 4, jnp.broadcast_to(query_norm, (8, 128)), key_norm)
+
+    rounds = [[(0, sibling)], [], [], []]
+    for d in range(1, 4):
+        rounds[1].append((d, (ctx_of(plane, y, (x + d) % 4), head)))
+        rounds[2].append((3 + d, (ctx_of(plane, (y + d) % 4, x), head)))
+    for dz in range(1, 8):
+        z = (half * 4 + plane + dz) % 8
+        rounds[3].append((6 + dz, (ctx_of(z % 4, y, x), (z // 4) * 2 + core)))
+
+    def stat_copy(r, n, target):
+        return remote(stat_own.at[r], stat_in.at[n], stat_send.at[n], stat_sem.at[n], target)
+
+    def stat_start(r):
+        for n, target in rounds[r]:
+            stat_copy(r, n, target).start()
+
+    def stat_finish(r):
+        best = stat_own[r]
+        for n, target in rounds[r]:
+            stat_copy(r, n, target).wait()
+            best = jnp.maximum(best, stat_in[n])
+        stat_own[r + 1] = best
+
+    def sib_copy(row):
+        return remote(keyval.at[row], keyval.at[row], sib_send.at[row], row_sem.at[row], sibling)
+
+    def take_row(row):
+        @pl.when(row >= 0)
+        def _():
+            sib_copy(row).wait_recv()
+
+            @pl.when(receiver)
+            def _():
+                sib_copy(row).start()
+
+    key_rank = lax.broadcasted_iota(jnp.int32, (block, 128), 0)
+
+    def absorb_keys(slot, keys, values_t, masks):
+        columns = pl.ds(pl.multiple_of(slot * slot_columns, 128), slot_columns)
+        scores = jnp.dot(keys, q_cols[:, columns], preferred_element_type=jnp.float32)
+        visible = jnp.concatenate(masks, axis=0)
+        visible = jnp.concatenate([visible] * (slot_columns // 128), axis=1)
+        weights = jnp.where(visible, jnp.exp2(scores * exponent_scale), 0.0)
+        denom[:, columns] += jnp.sum(weights.reshape(-1, 8, slot_columns), axis=0)
+        acc[:, columns] += jnp.dot(
+            values_t, weights.astype(jnp.bfloat16), preferred_element_type=jnp.float32
+        )
+
+    def turned_values(tile):
+        return jnp.concatenate([tile[:128], tile[128:]], axis=1)
+
+    def full_row(row, slot):
+        begin = begins[slot][:1]
+        absorb_keys(
+            slot,
+            keyval[row, 0].reshape(row_keys, head_depth),
+            jnp.concatenate([turned_values(keyval[row, 1, i]) for i in range(4)], axis=1),
+            [key_rank + (row * row_keys + i * block) >= begin for i in range(4)],
+        )
+
+    def edge_rows(slot):
+        slot_y, slot_x = yhi * 2 + slot // 2, (x // 2) * 2 + slot % 2
+        near = plane * 4 + slot_y
+        far = near - 8
+        held = jnp.maximum(far, 0) * (far >= 0).astype(jnp.int32) + near * (far < 0).astype(jnp.int32)
+        begin = begins[slot][:1]
+        position = slot_position(slot) + lane[:1]
+        keys, values_t, masks = [], [], []
+        for i in range(4):
+            is_near = (slot_x >= i).astype(jnp.int32)
+            row = is_near * near + (1 - is_near) * held
+            first = (is_near * near + (1 - is_near) * far) * row_keys + i * block
+            keys.append(keyval[row, 0, i])
+            values_t.append(turned_values(keyval[row, 1, i]))
+            key = key_rank + first
+            masks.append((key >= begin) & (key <= position))
+        absorb_keys(slot, jnp.concatenate(keys, axis=0), jnp.concatenate(values_t, axis=1), masks)
+
+        @pl.when(far >= 0)
+        def _():
+            first = far * row_keys + slot_x * block
+            absorb_keys(
+                slot,
+                keyval[held, 0, slot_x],
+                turned_values(keyval[held, 1, slot_x]),
+                [key_rank + first >= begin],
+            )
+
+    take_row(quad_row)
+
+    @pl.loop(2, 4)
+    def _(slot):
+        full_row(quad_row, slot)
+
+    stat_start(0)
+    take_row(quad_row + 1)
+    relay(0, 2)
+    relay(1, 2)
+    for t in range(1, 7):
+        row = quad_row - t
+        take_row(row)
+
+        @pl.when(row >= 0)
+        def _():
+            @pl.loop(0, 4)
+            def _(slot):
+                full_row(row, slot)
+
+        if t <= 4:
+            stat_finish(t - 1)
+            if t < 4:
+                stat_start(t)
+    stat_ref[...] = stat_own[4]
+    take_row(quad_row - 7)
+    take_row(quad_row - 8)
+
+    def o_copy(k):
+        my, mx = mate(k)
+        columns = pl.ds(pl.multiple_of(group * group_columns, 128), group_columns)
+        return remote(
+            o_part.at[my * 2 + mx],
+            out_ref.at[:, columns],
+            o_send.at[k],
+            o_sem.at[k],
+            (ctx_of(plane, yhi * 2 + my, (x // 2) * 2 + mx), head),
+        )
+
+    for k in (3, 2, 1, 0):
+        my, mx = mate(k)
+        slot = my * 2 + mx
+
+        @pl.when((my == 0) & (quad_row >= 7))
+        def _():
+            full_row(quad_row - 7, slot)
+
+        edge_rows(slot)
+
+        for pair in range(8):
+            columns = pl.ds(pl.multiple_of(slot * slot_columns + pair * 128, 128), 128)
+            share = acc[:, columns] / jnp.sum(denom[:, columns], axis=0, keepdims=True)
+            back = share.T.astype(jnp.bfloat16)
+            if k:
+                o_part[slot, :, pl.ds(pair * 256, 128)] = back[:own_tokens]
+                o_part[slot, :, pl.ds(pair * 256 + 128, 128)] = back[own_tokens:]
+            else:
+                at = pl.multiple_of(group * group_columns + pair * 256, 128)
+                out_ref[:, pl.ds(at, 128)] = back[:own_tokens]
+                out_ref[:, pl.ds(pl.multiple_of(at + 128, 128), 128)] = back[own_tokens:]
+        if k:
+            o_copy(k).start()
+
+    for k in (1, 2, 3):
+        q_copy(k).wait_send()
+    for n, (flip, ahead) in enumerate(z_plan):
+        pl.when(plane + ahead < 4)(lambda n=n, f=flip, a=ahead: z_copy(n, f, a).wait_send())
+    for flip in range(2):
+        for back in range(3):
+            plane_copies(flip, back, "wait")
+    for t in range(-1, 9):
+        row = quad_row - t
+
+        @pl.when((row >= 0) & receiver)
+        def _():
+            sib_copy(row).wait_send()
+
+    for k in (3, 2, 1):
+        o_copy(k).wait()
+
+
+def attend(queries, keys, values, doc_lengths):
+    vmem = pl.BlockSpec(memory_space=pltpu.VMEM)
+    smem = pl.BlockSpec(memory_space=pltpu.SMEM)
+    elements = 9 * row_keys * 4 * slot_columns
+    dma = pltpu.SemaphoreType.DMA
+    return pl.pallas_call(
+        attend_kernel,
+        name="attend",
+        out_shape=(
+            jax.ShapeDtypeStruct(queries.shape, jnp.bfloat16),
+            jax.ShapeDtypeStruct((8, 128), jnp.float32),
+        ),
+        in_specs=[vmem, vmem, vmem, smem],
+        out_specs=(vmem, vmem),
+        scratch_shapes=[
+            pltpu.VMEM((8, 2, block, head_depth), jnp.bfloat16),
+            pltpu.VMEM((16, 2, 4, block, head_depth), jnp.bfloat16),
+            pltpu.VMEM((4, own_tokens, group_columns), jnp.bfloat16),
+            pltpu.VMEM((head_depth, 4 * slot_columns), jnp.bfloat16),
+            pltpu.VMEM((head_depth, 4 * slot_columns), jnp.float32),
+            pltpu.VMEM((8, 4 * slot_columns), jnp.float32),
+            pltpu.VMEM((4, 8, 128), jnp.int32),
+            pltpu.VMEM((4, own_tokens, group_columns), jnp.bfloat16),
+            pltpu.VMEM((5, 8, 128), jnp.float32),
+            pltpu.VMEM((14, 8, 128), jnp.float32),
+            dma((8,)),
+            dma((16,)),
+            dma((4,)),
+            dma((4,)),
+            dma((14,)),
+            dma((6,)),
+            dma((24,)),
+            dma((4,)),
+            dma((16,)),
+            dma((4,)),
+            dma((14,)),
+        ],
+        compiler_params=pltpu.CompilerParams(
+            collective_id=0, has_side_effects=True, vmem_limit_bytes=56 << 20
+        ),
+        cost_estimate=pl.CostEstimate(
+            flops=4 * elements * head_depth, bytes_accessed=4 << 20, transcendentals=elements
+        ),
+    )(queries, keys, values, doc_lengths)
 def token_begins(doc_starts, positions):
     hit = doc_starts[None, :] <= positions[:, None]
     return jnp.max(jnp.where(hit, doc_starts[None, :], 0), axis=1)
@@ -74,7 +510,7 @@
     return (jnp.stack(new_tops), jnp.stack(new_denoms), jnp.stack(new_runs))
 
 
-def per_device(queries, keys, values, doc_lengths):
+def any_size(queries, keys, values, doc_lengths):
     by_head = lax.all_to_all(queries, "head", split_axis=1, concat_axis=0, tiled=True)
     tok_dev = by_head.shape[0]
     head_depth = keys.shape[1]
@@ -110,6 +546,20 @@
     return lax.all_to_all(merged, "head", split_axis=0, concat_axis=1, tiled=True)
 
 
+def per_device(queries, keys, values, doc_lengths):
+    out, norms = attend(queries, keys, values, doc_lengths)
+    bound = jnp.max(norms[:4]) * jnp.max(norms[4:]) * exponent_scale**2
+    return lax.cond(
+        bound <= safe_exponent**2,
+        lambda *_: out,
+        any_size,
+        queries,
+        keys,
+        values,
+        doc_lengths,
+    )
+
+
 def solution(mesh):
     in_specs = (P(("ctx", "head"), None), P("ctx", "head"), P("ctx", "head"), P())
     out_specs = P(("ctx", "head"), None)

time: 1240 us -> 1380 us (1.11)
  the two profiles are of different devices: /device:TPU:60 before, /device:TPU:118 now
where the time goes in v1:
time: 1380 us
  waiting for transfers between devices  683 us (49%)
  matrix products  340 us (25%)
  other arithmetic  141 us (10%)
  Pallas kernels  90 us (7%)
  local copies, waits for them, and re-layouts  61.6 us (4%)
  blocking collectives  24.4 us (2%)
  loops' own time  17.6 us (1%)
  between operations  14.6 us (1%)
    all_gather x1, waiting for transfers between devices, any_size(): lax.all_gather(values, 'ctx', axis=0, tiled=True)  355 us
    all_gather x1, waiting for transfers between devices, any_size(): lax.all_gather(keys, 'ctx', axis=0, tiled=True)  313 us
    dot_general x128, matrix products, add_block(): jnp.dot(weights.astype(jnp.bfloat16), value_block, preferred_element_type...  181 us
    dot_general x128, matrix products, add_block(): lax.dot_general(tile_query, key_block, (((1,), (1,)), ((), ())), preferre...  160 us
    add x132, other arithmetic, absorb(): positions = tile_start + jnp.arange(tok_rows, dtype=jnp.int32)  90.1 us
    pallas_call x1, Pallas kernels, attend(): pl.pallas_call(attend_kernel, name='attend', out_shape=(jax.ShapeDtypeStr...  90 us
    reshape x128, local copies, waits for them, and re-layouts, add_block(): visible = jnp.repeat(visible, group_size, axis=0)  44 us
    reduce_sum x128, other arithmetic, add_block(): denominator = denominator * rescale + jnp.sum(weights, axis=1)  34 us
  transfers between devices with their start and end apart: 3, of which 3 were waited for; matrix products, arithmetic and copies ran while one was open for 1% of the time, Pallas kernels for 0%

profile of v1, /device:TPU:118, one launch (start us, length us, event | category | flops | bytes accessed | tf_op | source)
XLA Modules:
  0.0 1376.9 jit_solution(7593769567817675407)
XLA Ops:
  6.5 90.0 %attend.1 = (bf16[64,8192]{1,0:T(8,128)(2,1)}, f32[8,128]{1,0:T(8,128)}) custom-call(bf16[64,8192]{1,0:T(8,128)(2,1)} %q_ref.1, bf16[256,128]{1,0:T(8,128)(2,1)} %k_ref.1, bf16[256,128]{1,0:T(8,128)(2,1)} %v_ref.1, s32[8]{0:T(128)} %len_ref.1), custom_call_target="tpu_custom_call" | custom-call | flops 19327352832 | bytes 4194304 | tf_op jit(solution)/shard_map/attend/pallas_call | solution.py:409
  99.1 1268.7 %conditional.1 = (bf16[64,8192]{1,0:T(8,128)(2,1)}) conditional(s32[]{:T(128)} %convert_element_type.35, (s32[8]{0:T(128)S(1)}, bf16[256,128]{1,0:T(8,128)(2,1)}, bf16[256,128]{1,0:T(8,128)(2,1)}, bf16[64,8192]{1,0:T(8,128)(2,1)S(1)}) %tuple.254, bf16[64,8192]{1,0:T(8,128)(2,1)} %get-tuple-element.456), branch_computations={%region_2.44_spmd, %region_44.45_spmd} | conditional | flops 1095125504 | bytes 104852736 | solution.py:552
  101.6 4.5 all-to-all-start
  118.5 14.0 %all-to-all-done = bf16[64,4,2048]{2,0,1:T(8,128)(2,1)S(1)} async-done(((bf16[64,4,2048]{2,0,1:T(8,128)(2,1)}), bf16[64,4,2048]{2,0,1:T(8,128)(2,1)S(1)}, u32[]{:S(2)}, u32[]{:S(2)}) %all-to-all-start) | async-done | bytes 1048608 | tf_op jit(solution)/shard_map/cond/branch_0_fun/all_to_all | solution.py:514
  133.1 312.9 %all-gather.3.cloned.1.call-done = bf16[16384,128]{1,0:T(8,128)(2,1)} async-done(((bf16[256,128]{1,0:T(8,128)(2,1)}), bf16[16384,128]{1,0:T(8,128)(2,1)}) %all-gather.3.cloned.1.call-update) | async-done | bytes 4194320 | tf_op jit(solution)/shard_map/cond/branch_0_fun/all_gather | solution.py:531
  446.0 354.6 %all-gather.5.cloned.1.call-done = bf16[16384,128]{1,0:T(8,128)(2,1)} async-done(((bf16[256,128]{1,0:T(8,128)(2,1)}), bf16[16384,128]{1,0:T(8,128)(2,1)}) %all-gather.5.cloned.1.call-update) | async-done | bytes 4194320 | tf_op jit(solution)/shard_map/cond/branch_0_fun/all_gather | solution.py:532
  800.6 67.6 %while.113 = (s32[]{:T(128)}, f32[512]{0:T(512)S(1)}, f32[512]{0:T(512)S(1)}, f32[512,128]{1,0:T(8,128)S(1)}, s32[]{:T(128)}, /*index=5*/s32[32]{0:T(128)S(1)}, ...) while((s32[]{:T(128)}, f32[512]{0:T(512)S(1)}, ...), condition=%wide.region_13.13_spmd.clone, body=%wide.region_10.12_spmd.clone.sunk | while | flops 136758816 | bytes 5706307 | solution.py:501
  803.4 1.4 convolution_add_fusion.17
  807.6 1.4 convolution_add_fusion.17
  868.2 67.4 %while.114 = (s32[]{:T(128)}, f32[512]{0:T(512)S(1)}, f32[512]{0:T(512)S(1)}, f32[512,128]{1,0:T(8,128)S(1)}, s32[]{:T(128)}, /*index=5*/s32[32]{0:T(128)S(1)}, ...) while((s32[]{:T(128)}, f32[512]{0:T(512)S(1)}, ...), condition=%wide.region_18.18_spmd.clone, body=%wide.region_15.17_spmd.clone.sunk | while | flops 136758816 | bytes 5706307 | solution.py:501
  871.0 1.4 convolution_add_fusion.18
  879.5 1.4 convolution_add_fusion.18
  887.9 1.4 convolution_add_fusion.18
  896.3 1.4 convolution_add_fusion.18
  904.7 1.4 convolution_add_fusion.18
  935.7 67.6 %while.115 = (s32[]{:T(128)}, f32[512]{0:T(512)S(1)}, f32[512]{0:T(512)S(1)}, f32[512,128]{1,0:T(8,128)S(1)}, s32[]{:T(128)}, /*index=5*/s32[32]{0:T(128)S(1)}, ...) while((s32[]{:T(128)}, f32[512]{0:T(512)S(1)}, ...), condition=%wide.region_23.23_spmd.clone, body=%wide.region_20.22_spmd.clone.sunk | while | flops 136758816 | bytes 5706307 | solution.py:501
  1003.4 66.6 %while.116 = (s32[]{:T(128)}, f32[512]{0:T(512)S(1)}, f32[512]{0:T(512)S(1)}, f32[512,128]{1,0:T(8,128)S(1)}, s32[]{:T(128)}, /*index=5*/s32[32]{0:T(128)S(1)}, ...) while((s32[]{:T(128)}, f32[512]{0:T(512)S(1)}, ...), condition=%wide.region_28.28_spmd.clone, body=%wide.region_25.27_spmd.clone.sunk | while | flops 136758816 | bytes 5706307 | solution.py:501
  1070.0 66.5 %while.117 = (s32[]{:T(128)}, f32[512]{0:T(512)S(1)}, f32[512]{0:T(512)S(1)}, f32[512,128]{1,0:T(8,128)S(1)}, s32[]{:T(128)}, /*index=5*/s32[32]{0:T(128)S(1)}, ...) while((s32[]{:T(128)}, f32[512]{0:T(512)S(1)}, ...), condition=%wide.region_33.33_spmd.clone, body=%wide.region_30.32_spmd.clone.sunk | while | flops 136758816 | bytes 5706307 | solution.py:501
  1136.6 67.4 %while.118 = (s32[]{:T(128)}, f32[512]{0:T(512)S(1)}, f32[512]{0:T(512)S(1)}, f32[512,128]{1,0:T(8,128)S(1)}, s32[]{:T(128)}, /*index=5*/s32[32]{0:T(128)S(1)}, ...) while((s32[]{:T(128)}, f32[512]{0:T(512)S(1)}, ...), condition=%wide.region_38.38_spmd.clone, body=%wide.region_35.37_spmd.clone.sunk | while | flops 136758816 | bytes 5706307 | solution.py:501
  1204.0 66.7 %while.119 = (s32[]{:T(128)}, f32[512]{0:T(512)S(1)}, f32[512]{0:T(512)S(1)}, f32[512,128]{1,0:T(8,128)S(1)}, s32[]{:T(128)}, /*index=5*/s32[32]{0:T(128)S(1)}, ...) while((s32[]{:T(128)}, f32[512]{0:T(512)S(1)}, ...), condition=%wide.region_43.43_spmd.clone, body=%wide.region_40.42_spmd.clone.sunk | while | flops 136758816 | bytes 5706307 | solution.py:501
  1270.7 67.4 %while.112 = (s32[]{:T(128)}, f32[512]{0:T(512)S(1)}, f32[512]{0:T(512)S(1)}, f32[512,128]{1,0:T(8,128)S(1)}, s32[]{:T(128)}, /*index=5*/s32[32]{0:T(128)S(1)}, ...) while((s32[]{:T(128)}, f32[512]{0:T(512)S(1)}, ...), condition=%wide.region_8.8_spmd.clone, body=%wide.region_5.7_spmd.clone.sunk | while | flops 136758816 | bytes 5706307 | solution.py:501
  1339.7 2.0 divide_convert_fusion
  1342.2 24.4 %all_to_all.26 = bf16[4,64,2048]{2,1,0:T(8,128)(2,1)S(1)} all-to-all(bf16[4,64,2048]{2,1,0:T(8,128)(2,1)S(1)} %convert_element_type.33), channel_id=1, replica_groups=mesh['ctx'=64,'head'=4] {'head'}, dimensions={0} | all-to-all | bytes 2097152 | tf_op jit(solution)/shard_map/cond/branch_0_fun/all_to_all | solution.py:546
  1367.8 2.3 copy.230
  (1459 shorter events, 530.1 us)
Async XLA Ops:
  6.5 92.5 %copy-start.1 = (bf16[64,8192]{1,0:T(8,128)(2,1)S(1)}, bf16[64,8192]{1,0:T(8,128)(2,1)}, u32[]{:S(2)}) copy-start(bf16[64,8192]{1,0:T(8,128)(2,1)} %q_ref.1) | copy-start | bytes 3145732
  6.5 92.6 %copy-start.2 = (s32[8]{0:T(128)S(1)}, s32[8]{0:T(128)}, u32[]{:S(2)}) copy-start(s32[8]{0:T(128)} %len_ref.1) | copy-start | bytes 100
  99.1 346.9 %all-gather.3.cloned.1.call-start = ((), (), s32[]{:S(2)}) async-start(), calls=%async_computation.2 | async-start | bytes 4259840 | tf_op jit(solution)/shard_map/cond/branch_0_fun/all_gather | solution.py:531
  99.8 700.7 %all-gather.5.cloned.1.call-start = ((), (), s32[]{:S(2)}) async-start(), calls=%async_computation.3 | async-start | bytes 4259840 | tf_op jit(solution)/shard_map/cond/branch_0_fun/all_gather | solution.py:532
  101.6 30.8 %all-to-all-start = ((bf16[64,4,2048]{2,0,1:T(8,128)(2,1)}), bf16[64,4,2048]{2,0,1:T(8,128)(2,1)S(1)}, u32[]{:S(2)}, u32[]{:S(2)}) async-start(bf16[64,4,2048]{2,0,1:T(8,128)(2,1)} %bitcast.106), calls=%async_computation | async-start | bytes 2097152 | tf_op jit(solution)/shard_map/cond/branch_0_fun/all_to_all | solution.py:514
  1338.4 1.4 copy-start
Sparse Core Ops, SparseCore 0:
  101.7 344.1 all-gather.2
  447.7 352.7 all-gather.4

commit v2 on v1

v2 whole, which is shorter than its diff:
```python
import math

import jax
import jax.numpy as jnp
from jax import lax
from jax.experimental import pallas as pl
from jax.experimental.pallas import tpu as pltpu
from jax.sharding import PartitionSpec as P

neg_big = -1e30
block_keys = 512
MESH = pl.DeviceIdType.MESH

head_depth = 128
heads_per_group = 16
group_columns = heads_per_group * head_depth
own_tokens = 64
block = 256
row_keys = 4 * block
slot_columns = own_tokens * heads_per_group
exponent_scale = math.log2(math.e) / math.sqrt(head_depth)
safe_exponent = 100.0


def attend_kernel(
    q_ref,
    k_ref,
    v_ref,
    len_ref,
    out_ref,
    bound_ref,
    stage,
    keyval,
    q_in,
    q_cols,
    acc,
    denom,
    begins,
    o_part,
    stat_own,
    stat_in,
    stage_sem,
    chunk_sem,
    q_sem,
    o_sem,
    stat_sem,
    z_send,
    entry_send,
    x_send,
    y_send,
    q_send,
    sib_send,
    o_send,
    stat_send,
    own_sem,
):
    ctx = lax.axis_index("ctx")
    head = lax.axis_index("head")
    plane, y, x = ctx // 16, (ctx // 4) % 4, ctx % 4
    half, core = head // 2, head % 2
    yhi, xhi, ylo, xlo = y // 2, x // 2, y % 2, x % 2
    ybit, xbit = (ylo + yhi) % 2, (xlo + xhi) % 2
    group = ybit * 2 + xbit
    quad_row = plane * 4 + yhi * 2
    quad_pair = plane * 2 + yhi
    receiver = core == xbit
    same = (ybit == half).astype(jnp.int32)

    def ctx_of(p, yy, xx):
        return p * 16 + yy * 4 + xx

    sibling = (ctx, half * 2 + 1 - core)
    partners = [sibling, (ctx_of(plane, yhi * 2 + 1 - ylo, xhi * 2 + 1 - xlo), head)]
    for d in range(1, 4):
        partners.append((ctx_of(plane, y, (x + d) % 4), head))
        partners.append((ctx_of(plane, (y + d) % 4, x), head))
    for dz in range(1, 8):
        z = (half * 4 + plane + dz) % 8
        partners.append((ctx_of(z % 4, y, x), (z // 4) * 2 + core))
    barrier = pltpu.get_barrier_semaphore()
    for partner in partners:
        pl.semaphore_signal(barrier, inc=1, device_id=partner, device_id_type=MESH)

    mine = half * 4 + plane
    stage[mine, 0] = k_ref[...]
    v_t = v_ref[...].T
    stage[mine, 1] = jnp.concatenate([v_t[:, :128], v_t[:, 128:]], axis=0)
    own_slot = ylo * 2 + xlo

    lane = lax.broadcasted_iota(jnp.int32, (8, 128), 1) % own_tokens
    starts = []
    total = jnp.int32(0)
    for d in range(8):
        starts.append(total)
        total = total + len_ref[d]

    def slot_position(slot):
        c = ctx_of(plane, yhi * 2 + slot // 2, xhi * 2 + slot % 2)
        return c * block + head * own_tokens

    for slot in range(4):
        position = slot_position(slot) + lane
        begin = jnp.zeros((8, 128), jnp.int32)
        for start in starts:
            begin = jnp.maximum(begin, jnp.where(position >= start, start, 0))
        begins[slot] = begin

    acc[...] = jnp.zeros_like(acc)
    denom[...] = jnp.zeros_like(denom)
    own_keys = k_ref[...].astype(jnp.float32)
    key_norm = jnp.max(jnp.sum(own_keys * own_keys, axis=1))

    def columns_of(slot, read):
        best = jnp.zeros((1, 128), jnp.float32)
        for pair in range(8):
            two = read(pair)
            tile = jnp.concatenate([two[:, :128], two[:, 128:]], axis=0)
            turned = tile.astype(jnp.float32).T
            best = jnp.maximum(best, jnp.sum(turned * turned, axis=0, keepdims=True))
            at = pl.multiple_of(slot * slot_columns + pair * 128, 128)
            q_cols[:, pl.ds(at, 128)] = turned.astype(jnp.bfloat16)
        return best

    def read_own(pair):
        at = pl.multiple_of(group * group_columns + pair * 256, 128)
        return q_ref[:, pl.ds(at, 256)]

    query_norm = columns_of(own_slot, read_own)

    pl.semaphore_wait(barrier, len(partners))

    def remote(src, dst, send, recv, target):
        return pltpu.make_async_remote_copy(
            src_ref=src,
            dst_ref=dst,
            send_sem=send,
            recv_sem=recv,
            device_id=target,
            device_id_type=MESH,
        )

    def z_copy(n, index, to_half, to_plane):
        return remote(
            stage.at[index],
            stage.at[index],
            z_send.at[n],
            stage_sem.at[index],
            (ctx_of(to_plane, y, x), to_half * 2 + core),
        )

    def stage_index(flip, back):
        return ((half + flip) % 2) * 4 + plane - back

    z_hops = [
        (plane <= 3, 0, mine, 1 - half, jnp.minimum(plane + 1, 3)),
        (plane <= 2, 1, mine, half, plane + 1),
        (plane >= 1, 2, stage_index(1, 1), half, plane - 1),
        ((plane >= 1) & (plane <= 2), 3, stage_index(1, 1), half, plane + 1),
        ((plane >= 1) & (plane <= 2), 4, stage_index(0, 1), half, plane + 1),
    ]

    def z_start(n):
        pl.when(z_hops[n][0])(lambda: z_copy(*z_hops[n][1:]).start())

    def entry(flip, back, act):
        g = (half + flip) % 2
        p = plane - back
        index = stage_index(flip, back)
        to_y, to_x = yhi * 2 + (g + yhi) % 2, xhi * 2 + (core + xhi) % 2
        here = (to_y == y) & (to_x == x)
        pair = p * 2 + yhi
        target = keyval.at[pair, xhi, ylo, :, xlo]

        @pl.when((p >= 0) & jnp.logical_not(here))
        def _():
            copy = remote(
                stage.at[index],
                target,
                entry_send.at[flip * 3 + back],
                chunk_sem.at[pair * 2 + xhi],
                (ctx_of(plane, to_y, to_x), head),
            )
            copy.start() if act == "start" else copy.wait_send()

        if act == "start":

            @pl.when((p >= 0) & here)
            def _():
                pltpu.make_async_copy(
                    stage.at[index], target, chunk_sem.at[pair * 2 + xhi]
                ).start()

    def relay(flip, back, *hops):
        @pl.when(plane >= back)
        def _():
            z_copy(0, stage_index(flip, back), 1 - half, plane).wait_recv()

        for hop in hops:
            z_start(hop)
        entry(flip, back, "start")

    def mate(k):
        my, mx = (ylo + k // 2) % 2, (xlo + k % 2) % 2
        return my, mx

    def q_copy(k):
        my, mx = mate(k)
        to_group = ((my + yhi) % 2) * 2 + (mx + xhi) % 2
        columns = pl.ds(pl.multiple_of(to_group * group_columns, 128), group_columns)
        return remote(
            q_ref.at[:, columns],
            q_in.at[own_slot],
            q_send.at[k],
            q_sem.at[own_slot],
            (ctx_of(plane, yhi * 2 + my, xhi * 2 + mx), head),
        )

    def q_wait(k):
        my, mx = mate(k)
        slot = my * 2 + mx
        remote(q_in.at[slot], q_in.at[slot], q_send.at[0], q_sem.at[slot], sibling).wait_recv()

    z_start(0)
    z_start(1)
    entry(0, 0, "start")
    for k in (1, 2, 3):
        q_copy(k).start()

    def chunk_copy(pair, side, send, target):
        chunk = keyval.at[pair, side]
        return remote(chunk, chunk, send, chunk_sem.at[pair * 2 + side], target)

    def sib_copy(pair, side):
        return chunk_copy(pair, side, sib_send.at[pair * 2 + side], sibling)

    x_next = (ctx_of(plane, y, (1 - xhi) * 2 + (xbit + 1 - xhi) % 2), head)
    y_next = (ctx_of(plane, (1 - yhi) * 2 + (ybit + 1 - yhi) % 2, x), head)

    def sent_on(back):
        return ((back == 0) & (yhi == 0)) | (back == 1) | ((back == 2) & (yhi == 1))

    def got_from(back):
        return ((back == 0) & (yhi == 1)) | (back == 1) | ((back == 2) & (yhi == 0))

    def x_copy(back):
        return chunk_copy((plane - back) * 2 + yhi, xhi, x_send.at[back], x_next)

    def y_copy(back, side):
        pair = (plane - back) * 2 + yhi
        return chunk_copy(pair, (xhi + side) % 2, y_send.at[back * 2 + side], y_next)

    def take_own(back):
        pair = (plane - back) * 2 + yhi

        @pl.when(plane >= back)
        def _():
            sib_copy(pair, xhi).wait_recv()

            @pl.when(receiver)
            def _():
                x_copy(back).start()
                pl.when(sent_on(back))(lambda: y_copy(back, 0).start())
                sib_copy(pair, xhi).start()

    def take_x(back):
        pair = (plane - back) * 2 + yhi

        @pl.when(plane >= back)
        def _():
            sib_copy(pair, 1 - xhi).wait_recv()

            @pl.when(receiver)
            def _():
                pl.when(sent_on(back))(lambda: y_copy(back, 1).start())
                sib_copy(pair, 1 - xhi).start()

    def take_y(back, side):
        pair = (plane - back) * 2 + 1 - yhi

        @pl.when((plane >= back) & got_from(back))
        def _():
            sib_copy(pair, (xhi + side) % 2).wait_recv()
            pl.when(receiver)(lambda: sib_copy(pair, (xhi + side) % 2).start())

    near_half = same == 1
    relay(0, 1, 4)
    pl.when(near_half)(lambda: take_own(0))
    relay(0, 2)
    relay(1, 1, 2, 3)
    take_own(1)

    def norms(query_norm):
        rank = lax.broadcasted_iota(jnp.int32, (8, 128), 0)
        return jnp.where(rank < 4, jnp.broadcast_to(query_norm, (8, 128)), key_norm)

    stat_own[0] = norms(query_norm)

    def slot_of(k):
        my, mx = mate(k)
        return my * 2 + mx

    def take_queries(k):
        q_wait(k)
        slot = slot_of(k)
        best = columns_of(slot, lambda pair: q_in[slot, :, pl.ds(pair * 256, 256)])
        stat_own[0] = jnp.maximum(stat_own[0], norms(best))

    rounds = [[(0, sibling)], [], [], []]
    for d in range(1, 4):
        rounds[1].append((d, (ctx_of(plane, y, (x + d) % 4), head)))
        rounds[2].append((3 + d, (ctx_of(plane, (y + d) % 4, x), head)))
    for dz in range(1, 8):
        z = (half * 4 + plane + dz) % 8
        rounds[3].append((6 + dz, (ctx_of(z % 4, y, x), (z // 4) * 2 + core)))

    def stat_copy(r, n, target):
        return remote(stat_own.at[r], stat_in.at[n], stat_send.at[n], stat_sem.at[n], target)

    def stat_start(r):
        for n, target in rounds[r]:
            stat_copy(r, n, target).start()

    def stat_finish(r):
        best = stat_own[r]
        for n, target in rounds[r]:
            stat_copy(r, n, target).wait()
            best = jnp.maximum(best, stat_in[n])
        stat_own[r + 1] = best

    key_rank = lax.broadcasted_iota(jnp.int32, (block, 128), 0)

    def absorb_keys(slot, keys, values_t, masks):
        columns = pl.ds(pl.multiple_of(slot * slot_columns, 128), slot_columns)
        scores = jnp.dot(keys, q_cols[:, columns], preferred_element_type=jnp.float32)
        visible = jnp.concatenate(masks, axis=0)
        visible = jnp.concatenate([visible] * (slot_columns // 128), axis=1)
        weights = jnp.where(visible, jnp.exp2(scores * exponent_scale), 0.0)
        ones = jnp.ones((8, values_t.shape[1]), jnp.bfloat16)
        sums = jnp.dot(
            jnp.concatenate([values_t, ones], axis=0),
            weights.astype(jnp.bfloat16),
            preferred_element_type=jnp.float32,
        )
        acc[:, columns] += sums[:head_depth]
        denom[:, columns] += sums[head_depth:]

    def key_block(row, i):
        return keyval[row // 2, i // 2, row % 2, 0, i % 2]

    def value_block(row, i):
        tile = keyval[row // 2, i // 2, row % 2, 1, i % 2]
        return jnp.concatenate([tile[:128], tile[128:]], axis=1)

    def whole_blocks(slot, blocks):
        begin = begins[slot][:1]
        absorb_keys(
            slot,
            jnp.concatenate([key_block(row, i) for row, i in blocks], axis=0),
            jnp.concatenate([value_block(row, i) for row, i in blocks], axis=1),
            [key_rank + (row * row_keys + i * block) >= begin for row, i in blocks],
        )

    def full_row(row, slot):
        whole_blocks(slot, [(row, i) for i in range(4)])

    def full_chunk(pair, side, slot):
        blocks = [(pair * 2 + dy, side * 2 + dx) for dy in range(2) for dx in range(2)]
        whole_blocks(slot, blocks)

    def edge_rows(slot):
        slot_y, slot_x = yhi * 2 + slot // 2, xhi * 2 + slot % 2
        near = plane * 4 + slot_y
        far = near - 8
        there = (far >= 0).astype(jnp.int32)
        held = there * far + (1 - there) * near
        begin = begins[slot][:1]
        position = slot_position(slot) + lane[:1]
        keys, values_t, masks = [], [], []
        for i in range(4):
            is_near = (slot_x >= i).astype(jnp.int32)
            row = is_near * near + (1 - is_near) * held
            first = (is_near * near + (1 - is_near) * far) * row_keys + i * block
            keys.append(key_block(row, i))
            values_t.append(value_block(row, i))
            key = key_rank + first
            masks.append((key >= begin) & (key <= position))
        absorb_keys(slot, jnp.concatenate(keys, axis=0), jnp.concatenate(values_t, axis=1), masks)

        @pl.when(far >= 0)
        def _():
            first = far * row_keys + slot_x * block
            absorb_keys(
                slot,
                key_block(held, slot_x),
                value_block(held, slot_x),
                [key_rank + first >= begin],
            )

    def when_near(act, near):
        pl.when(same == near)(act)

    far_steps = {('relay', 0): 1, ('relay', 2): 2, ('own', 0): 4, ('own', 2): 5, ('x', 1): 4, ('y', 1, 0): 7, ('y', 1, 1): 11, ('x', 0): 13, ('x', 2): 14, ('y', 0, 0): 18, ('y', 2, 0): 18}
    near_steps = {('x', 0): 1, ('own', 2): 2, ('x', 1): 3, ('relay', 0): 4, ('relay', 2): 4, ('x', 2): 7, ('y', 1, 0): 7, ('y', 1, 1): 11, ('y', 0, 0): 18, ('y', 2, 0): 18}
    last_keys = [('y', 0, 1), ('y', 2, 1)]
    stat_steps = [6, 10, 15, 20]
    events = []
    for key, at in far_steps.items():
        events.append((at, 0, key))
    for key, at in near_steps.items():
        events.append((at, 1, key))

    def act_on(key):
        kind, back = key[0], key[1]
        if kind == "relay":
            relay(1, back)
        elif kind == "own":
            take_own(back)
        elif kind == "x":
            take_x(back)
        else:
            take_y(back, key[2])

    def before(step, at):
        here = [(near, key) for when, near, key in events if when == at]
        starts_here = [r for r in range(4) if stat_steps[r] == at]
        if here or starts_here or 1 <= at <= 3:

            @pl.when(step == at)
            def _():
                if 1 <= at <= 3:
                    take_queries(at)
                for near, key in here:
                    when_near(lambda key=key: act_on(key), near)
                for r in starts_here:
                    if r:
                        stat_finish(r - 1)
                    stat_start(r)

    first_y = yhi * -3 + (1 - yhi) * -1

    def chunk_step(chunk, k):
        side = (xhi + chunk) % 2
        order = chunk // 2
        back = jnp.where(order == 0, -2, jnp.where(order == 1, first_y, -4 - first_y))
        pair = quad_pair + back

        @pl.when(pair >= 0)
        def _():
            full_chunk(pair, side, slot_of(k))

    @pl.loop(0, 16)
    def _(step):
        for at in range(16):
            before(step, at)
        chunk_step(step // 4, step % 4)

    @pl.loop(16, 20)
    def _(step):
        for at in range(16, 20):
            before(step, at)
        slot = slot_of(step - 16)
        last = quad_row - 7 * (1 - slot // 2)

        @pl.when(last >= 0)
        def _():
            full_row(last, slot)

        edge_rows(slot)

    @pl.loop(20, 24)
    def _(step):
        for at in range(20, 24):
            before(step, at)
        chunk_step(jnp.int32(4), step - 20)

    for key in last_keys:
        act_on(key)
    def o_columns():
        return pl.ds(pl.multiple_of(group * group_columns, 128), group_columns)

    def o_copy(k):
        my, mx = mate(k)
        return remote(
            o_part.at[my * 2 + mx],
            out_ref.at[:, o_columns()],
            o_send.at[k],
            o_sem.at[k],
            (ctx_of(plane, yhi * 2 + my, xhi * 2 + mx), head),
        )

    def o_arrival(k):
        my, mx = mate(k)
        from_group = ((my + yhi) % 2) * 2 + (mx + xhi) % 2
        columns = pl.ds(pl.multiple_of(from_group * group_columns, 128), group_columns)
        return remote(
            o_part.at[own_slot], out_ref.at[:, columns], o_send.at[k], o_sem.at[k], sibling
        )

    for k in (3, 2, 1, 0):
        slot = slot_of(k)
        chunk_step(jnp.int32(5), jnp.int32(k))

        for pair in range(8):
            columns = pl.ds(pl.multiple_of(slot * slot_columns + pair * 128, 128), 128)
            share = acc[:, columns] / denom[:1, columns]
            back = share.T.astype(jnp.bfloat16)
            o_part[slot, :, pl.ds(pair * 256, 128)] = back[:own_tokens]
            o_part[slot, :, pl.ds(pair * 256 + 128, 128)] = back[own_tokens:]
        if k:
            o_copy(k).start()
    home = pltpu.make_async_copy(o_part.at[own_slot], out_ref.at[:, o_columns()], own_sem)
    home.start()
    stat_finish(3)
    bound_ref[0] = jnp.max(stat_own[4, :4]) * jnp.max(stat_own[4, 4:])

    for k in (1, 2, 3):
        q_copy(k).wait_send()
    for hop in z_hops:
        pl.when(hop[0])(lambda hop=hop: z_copy(*hop[1:]).wait_send())
    for flip in range(2):
        for back in range(3):
            entry(flip, back, "wait")
    for back in range(3):

        @pl.when((plane >= back) & receiver)
        def _():
            x_copy(back).wait_send()
            sib_copy((plane - back) * 2 + yhi, 0).wait_send()
            sib_copy((plane - back) * 2 + yhi, 1).wait_send()

            @pl.when(sent_on(back))
            def _():
                y_copy(back, 0).wait_send()
                y_copy(back, 1).wait_send()

            @pl.when(got_from(back))
            def _():
                sib_copy((plane - back) * 2 + 1 - yhi, 0).wait_send()
                sib_copy((plane - back) * 2 + 1 - yhi, 1).wait_send()

    for k in (3, 2, 1):
        o_copy(k).wait_send()
        o_arrival(k).wait_recv()
    home.wait()


def attend(queries, keys, values, doc_lengths):
    vmem = pl.BlockSpec(memory_space=pltpu.VMEM)
    smem = pl.BlockSpec(memory_space=pltpu.SMEM)
    elements = 9 * row_keys * 4 * slot_columns
    dma = pltpu.SemaphoreType.DMA
    return pl.pallas_call(
        attend_kernel,
        name="attend",
        out_shape=(
            jax.ShapeDtypeStruct(queries.shape, jnp.bfloat16),
            jax.ShapeDtypeStruct((1,), jnp.float32),
        ),
        in_specs=[vmem, vmem, vmem, smem],
        out_specs=(vmem, smem),
        scratch_shapes=[
            pltpu.VMEM((8, 2, block, head_depth), jnp.bfloat16),
            pltpu.VMEM((8, 2, 2, 2, 2, block, head_depth), jnp.bfloat16),
            pltpu.VMEM((4, own_tokens, group_columns), jnp.bfloat16),
            pltpu.VMEM((head_depth, 4 * slot_columns), jnp.bfloat16),
            pltpu.VMEM((head_depth, 4 * slot_columns), jnp.float32),
            pltpu.VMEM((8, 4 * slot_columns), jnp.float32),
            pltpu.VMEM((4, 8, 128), jnp.int32),
            pltpu.VMEM((4, own_tokens, group_columns), jnp.bfloat16),
            pltpu.VMEM((5, 8, 128), jnp.float32),
            pltpu.VMEM((14, 8, 128), jnp.float32),
            dma((8,)),
            dma((16,)),
            dma((4,)),
            dma((4,)),
            dma((14,)),
            dma((5,)),
            dma((6,)),
            dma((3,)),
            dma((6,)),
            dma((4,)),
            dma((16,)),
            dma((4,)),
            dma((14,)),
            dma,
        ],
        compiler_params=pltpu.CompilerParams(
            collective_id=0, has_side_effects=True, vmem_limit_bytes=56 << 20
        ),
        cost_estimate=pl.CostEstimate(
            flops=4 * elements * head_depth, bytes_accessed=4 << 20, transcendentals=elements
        ),
    )(queries, keys, values, doc_lengths)


def token_begins(doc_starts, positions):
    hit = doc_starts[None, :] <= positions[:, None]
    return jnp.max(jnp.where(hit, doc_starts[None, :], 0), axis=1)


def absorb(
    carried, held_tiles, tile_starts, doc_starts, key_piece, value_piece, piece_start, tok_rows
):
    top_scores, denominators, runnings = carried
    piece_rows = key_piece.shape[0]
    block_width = math.gcd(piece_rows, block_keys)
    tile_count, query_rows, head_depth = held_tiles.shape
    group_size = query_rows // tok_rows
    score_scale = 1.0 / math.sqrt(head_depth)
    new_tops, new_denoms, new_runs = ([], [], [])
    for tile_num in range(tile_count):
        tile_start = tile_starts[tile_num]
        positions = tile_start + jnp.arange(tok_rows, dtype=jnp.int32)
        begins = token_begins(doc_starts, positions)
        low_pos = jnp.maximum(begins[0], piece_start)
        high_pos = jnp.minimum(tile_start + tok_rows, piece_start + piece_rows)
        first_block = low_pos // block_width
        last_block = jnp.maximum(first_block, (high_pos + block_width - 1) // block_width)
        tile_query = held_tiles[tile_num]

        def add_block(block_index, loop_state):
            top_score, denominator, running = loop_state
            offset = block_index * block_width
            key_block = lax.dynamic_slice_in_dim(key_piece, offset, block_width, 0)
            value_block = lax.dynamic_slice_in_dim(value_piece, offset, block_width, 0)
            scores = (
                lax.dot_general(
                    tile_query,
                    key_block,
                    (((1,), (1,)), ((), ())),
                    preferred_element_type=jnp.float32,
                )
                * score_scale
            )
            key_pos = offset + jnp.arange(block_width, dtype=jnp.int32)
            visible = (key_pos[None, :] <= positions[:, None]) & (
                key_pos[None, :] >= begins[:, None]
            )
            visible = jnp.repeat(visible, group_size, axis=0)
            new_top = jnp.maximum(top_score, jnp.max(jnp.where(visible, scores, neg_big), axis=1))
            weights = jnp.where(visible, jnp.exp(scores - new_top[:, None]), 0.0)
            rescale = jnp.exp(top_score - new_top)
            denominator = denominator * rescale + jnp.sum(weights, axis=1)
            running = running * rescale[:, None] + jnp.dot(
                weights.astype(jnp.bfloat16), value_block, preferred_element_type=jnp.float32
            )
            return (new_top, denominator, running)

        result = lax.fori_loop(
            first_block,
            last_block,
            add_block,
            (top_scores[tile_num], denominators[tile_num], runnings[tile_num]),
        )
        new_tops.append(result[0])
        new_denoms.append(result[1])
        new_runs.append(result[2])
    return (jnp.stack(new_tops), jnp.stack(new_denoms), jnp.stack(new_runs))


def from_all(piece):
    copies = jnp.tile(piece, (lax.axis_size("ctx"), 1))
    return lax.all_to_all(copies, "ctx", split_axis=0, concat_axis=0, tiled=True)


def any_size(queries, keys, values, doc_lengths):
    by_head = lax.all_to_all(queries, "head", split_axis=1, concat_axis=0, tiled=True)
    tok_dev = by_head.shape[0]
    head_depth = keys.shape[1]
    group_size = by_head.shape[1] // head_depth
    tile_count = 8
    tok_rows = tok_dev // tile_count
    shard_index = lax.axis_index("ctx")
    doc_starts = jnp.cumsum(doc_lengths) - doc_lengths
    tile_query = by_head.reshape(tile_count, tok_rows * group_size, head_depth)
    tile_starts = shard_index * tok_dev + jnp.arange(tile_count, dtype=jnp.int32) * tok_rows
    query_rows = tok_rows * group_size
    initial = (
        jnp.full((tile_count, query_rows), neg_big, jnp.float32),
        jnp.zeros((tile_count, query_rows), jnp.float32),
        jnp.zeros((tile_count, query_rows, head_depth), jnp.float32),
    )
    whole_keys, whole_values = (
        from_all(keys),
        from_all(values),
    )
    carried = absorb(
        initial,
        tile_query,
        tile_starts,
        doc_starts,
        whole_keys,
        whole_values,
        jnp.int32(0),
        tok_rows,
    )
    results = (carried[2] / carried[1][..., None]).astype(jnp.bfloat16)
    merged = results.reshape(tok_dev, group_size * head_depth)
    return lax.all_to_all(merged, "head", split_axis=0, concat_axis=1, tiled=True)


def per_device(queries, keys, values, doc_lengths):
    out, bound = attend(queries, keys, values, doc_lengths)
    return lax.cond(
        bound[0] <= (safe_exponent / exponent_scale) ** 2,
        lambda *_: out,
        any_size,
        queries,
        keys,
        values,
        doc_lengths,
    )


def solution(mesh):
    in_specs = (P(("ctx", "head"), None), P("ctx", "head"), P("ctx", "head"), P())
    out_specs = P(("ctx", "head"), None)
    return jax.shard_map(
        per_device, mesh=mesh, in_specs=in_specs, out_specs=out_specs, check_vma=False
    )
```

time: 1380 us -> 897 us (0.65)
  the two profiles are of different devices: /device:TPU:118 before, /device:TPU:104 now
where the time goes in v2:
time: 897 us; the launch traced here: 891 us
  matrix products  340 us (38%)
  blocking collectives  157 us (18%)
  other arithmetic  134 us (15%)
  Pallas kernels  88.4 us (10%)
  waiting for transfers between devices  77.4 us (9%)
  local copies, waits for them, and re-layouts  64.6 us (7%)
  loops' own time  17.5 us (2%)
  starting transfers between devices  11 us (1%)
    dot_general x128, matrix products, add_block(): jnp.dot(weights.astype(jnp.bfloat16), value_block, preferred_element_type...  181 us
    dot_general x128, matrix products, add_block(): lax.dot_general(tile_query, key_block, (((1,), (1,)), ((), ())), preferre...  159 us
    all_to_all x1, blocking collectives, from_all(): lax.all_to_all(copies, 'ctx', split_axis=0, concat_axis=0, tiled=True)  109 us
    pallas_call x1, Pallas kernels, attend(): pl.pallas_call(attend_kernel, name='attend', out_shape=(jax.ShapeDtypeStr...  88.4 us
    add x132, other arithmetic, absorb(): positions = tile_start + jnp.arange(tok_rows, dtype=jnp.int32)  84.4 us
    all_to_all x1, waiting for transfers between devices, from_all(): lax.all_to_all(copies, 'ctx', split_axis=0, concat_axis=0, tiled=True)  77.4 us
    reshape x128, local copies, waits for them, and re-layouts, add_block(): visible = jnp.repeat(visible, group_size, axis=0)  44 us
    reduce_sum x128, other arithmetic, add_block(): denominator = denominator * rescale + jnp.sum(weights, axis=1)  34 us
  transfers between devices with their start and end apart: 1, of which 1 were waited for; matrix products, arithmetic and copies ran while one was open for 1% of the time, Pallas kernels for 0%

profile of v2, /device:TPU:104, one launch (start us, length us, event | category | flops | bytes accessed | tf_op | source)
XLA Modules:
  0.0 890.8 jit_solution(14765544718761458814)
XLA Ops:
  0.0 88.4 %attend.1 = (bf16[64,8192]{1,0:T(8,128)(2,1)}, f32[1]{0:T(128)}) custom-call(bf16[64,8192]{1,0:T(8,128)(2,1)} %q_ref.1, bf16[256,128]{1,0:T(8,128)(2,1)} %k_ref.1, bf16[256,128]{1,0:T(8,128)(2,1)} %v_ref.1, s32[8]{0:T(128)} %len_ref.1), custom_call_target="tpu_custom_call" | custom-call | flops 19327352832 | bytes 4194304 | tf_op jit(solution)/shard_map/attend/pallas_call | solution.py:552
  89.2 799.4 %conditional.1 = (bf16[64,8192]{1,0:T(8,128)(2,1)}) conditional(s32[]{:T(128)} %bitcast.54, (s32[8]{0:T(128)S(1)}, bf16[256,128]{1,0:T(8,128)(2,1)S(1)}, bf16[256,128]{1,0:T(8,128)(2,1)S(1)}, bf16[64,8192]{1,0:T(8,128)(2,1)S(1)}) %tuple.245, bf16[64,8192]{1,0:T(8,128)(2,1)} %get-tuple-element.456), branch_computations={%region_0.42_spmd, %region_42.43_spmd} | conditional | flops 1095125504 | bytes 107736240 | solution.py:704
  89.3 22.4 %all_to_all.40 = bf16[64,4,2048]{2,0,1:T(8,128)(2,1)S(1)} all-to-all(bf16[64,4,2048]{2,0,1:T(8,128)(2,1)S(1)} %bitcast.161), channel_id=1, replica_groups=mesh['ctx'=64,'head'=4] {'head'}, dimensions={1} | all-to-all | bytes 2097152 | tf_op jit(solution)/shard_map/cond/branch_0_fun/all_to_all | solution.py:667
  112.7 109.2 %all_to_all.41 = bf16[64,256,128]{2,1,0:T(8,128)(2,1)} all-to-all(bf16[64,256,128]{2,1,0:T(8,128)(2,1)S(1)} %tile.0), channel_id=1, replica_groups=mesh['ctx'=64,'head'=4] {'ctx'}, dimensions={0} | all-to-all | bytes 8388608 | tf_op jit(solution)/shard_map/cond/branch_0_fun/all_to_all | solution.py:663
  221.8 3.0 tile.1
  224.8 11.0 %all-to-all-start.2 = ((bf16[64,256,128]{2,1,0:T(8,128)(2,1)}), bf16[64,256,128]{2,1,0:T(8,128)(2,1)}, u32[]{:S(2)}, u32[]{:S(2)}) async-start(bf16[64,256,128]{2,1,0:T(8,128)(2,1)} %tile.1), calls=%async_computation.2 | async-start | bytes 8388608 | tf_op jit(solution)/shard_map/cond/branch_0_fun/all_to_all | solution.py:663
  248.1 77.4 %all-to-all-done.2 = bf16[64,256,128]{2,1,0:T(8,128)(2,1)} async-done(((bf16[64,256,128]{2,1,0:T(8,128)(2,1)}), bf16[64,256,128]{2,1,0:T(8,128)(2,1)}, u32[]{:S(2)}, u32[]{:S(2)}) %all-to-all-start.2) | async-done | bytes 4194336 | tf_op jit(solution)/shard_map/cond/branch_0_fun/all_to_all | solution.py:663
  325.5 66.4 %while.113 = (s32[]{:T(128)}, f32[512]{0:T(512)S(1)}, f32[512]{0:T(512)S(1)}, f32[512,128]{1,0:T(8,128)S(1)}, s32[]{:T(128)}, /*index=5*/s32[32]{0:T(128)S(1)}, ...) while((s32[]{:T(128)}, f32[512]{0:T(512)S(1)}, ...), condition=%wide.region_11.11_spmd.clone, body=%wide.region_8.10_spmd.clone.sunk | while | flops 136758816 | bytes 5706307 | solution.py:649
  392.0 67.6 %while.114 = (s32[]{:T(128)}, f32[512]{0:T(512)S(1)}, f32[512]{0:T(512)S(1)}, f32[512,128]{1,0:T(8,128)S(1)}, s32[]{:T(128)}, /*index=5*/s32[32]{0:T(128)S(1)}, ...) while((s32[]{:T(128)}, f32[512]{0:T(512)S(1)}, ...), condition=%wide.region_16.16_spmd.clone, body=%wide.region_13.15_spmd.clone.sunk | while | flops 136758816 | bytes 5706307 | solution.py:649
  459.7 66.7 %while.115 = (s32[]{:T(128)}, f32[512]{0:T(512)S(1)}, f32[512]{0:T(512)S(1)}, f32[512,128]{1,0:T(8,128)S(1)}, s32[]{:T(128)}, /*index=5*/s32[32]{0:T(128)S(1)}, ...) while((s32[]{:T(128)}, f32[512]{0:T(512)S(1)}, ...), condition=%wide.region_21.21_spmd.clone, body=%wide.region_18.20_spmd.clone.sunk | while | flops 136758816 | bytes 5706307 | solution.py:649
  466.6 1.4 convolution_add_fusion.19
  470.8 1.4 convolution_add_fusion.19
  475.0 1.4 convolution_add_fusion.19
  479.1 1.4 convolution_add_fusion.19
  483.3 1.4 convolution_add_fusion.19
  526.5 67.3 %while.116 = (s32[]{:T(128)}, f32[512]{0:T(512)S(1)}, f32[512]{0:T(512)S(1)}, f32[512,128]{1,0:T(8,128)S(1)}, s32[]{:T(128)}, /*index=5*/s32[32]{0:T(128)S(1)}, ...) while((s32[]{:T(128)}, f32[512]{0:T(512)S(1)}, ...), condition=%wide.region_26.26_spmd.clone, body=%wide.region_23.25_spmd.clone.sunk | while | flops 136758816 | bytes 5706307 | solution.py:649
  593.9 66.7 %while.117 = (s32[]{:T(128)}, f32[512]{0:T(512)S(1)}, f32[512]{0:T(512)S(1)}, f32[512,128]{1,0:T(8,128)S(1)}, s32[]{:T(128)}, /*index=5*/s32[32]{0:T(128)S(1)}, ...) while((s32[]{:T(128)}, f32[512]{0:T(512)S(1)}, ...), condition=%wide.region_31.31_spmd.clone, body=%wide.region_28.30_spmd.clone.sunk | while | flops 136758816 | bytes 5706307 | solution.py:649
  660.6 65.8 %while.118 = (s32[]{:T(128)}, f32[512]{0:T(512)S(1)}, f32[512]{0:T(512)S(1)}, f32[512,128]{1,0:T(8,128)S(1)}, s32[]{:T(128)}, /*index=5*/s32[32]{0:T(128)S(1)}, ...) while((s32[]{:T(128)}, f32[512]{0:T(512)S(1)}, ...), condition=%wide.region_36.36_spmd.clone, body=%wide.region_33.35_spmd.clone.sunk | while | flops 136758816 | bytes 5706307 | solution.py:649
  726.5 65.7 %while.119 = (s32[]{:T(128)}, f32[512]{0:T(512)S(1)}, f32[512]{0:T(512)S(1)}, f32[512,128]{1,0:T(8,128)S(1)}, s32[]{:T(128)}, /*index=5*/s32[32]{0:T(128)S(1)}, ...) while((s32[]{:T(128)}, f32[512]{0:T(512)S(1)}, ...), condition=%wide.region_41.41_spmd.clone, body=%wide.region_38.40_spmd.clone.sunk | while | flops 136758816 | bytes 5706307 | solution.py:649
  757.9 1.4 convolution_add_fusion.23
  792.2 65.7 %while.112 = (s32[]{:T(128)}, f32[512]{0:T(512)S(1)}, f32[512]{0:T(512)S(1)}, f32[512,128]{1,0:T(8,128)S(1)}, s32[]{:T(128)}, /*index=5*/s32[32]{0:T(128)S(1)}, ...) while((s32[]{:T(128)}, f32[512]{0:T(512)S(1)}, ...), condition=%wide.region_6.6_spmd.clone, body=%wide.region_3.5_spmd.clone.sunk | while | flops 136758816 | bytes 5706307 | solution.py:649
  859.5 2.0 divide_convert_fusion
  862.0 25.4 %all_to_all.42 = bf16[4,64,2048]{2,1,0:T(8,128)(2,1)S(1)} all-to-all(bf16[4,64,2048]{2,1,0:T(8,128)(2,1)S(1)} %convert_element_type.35), channel_id=1, replica_groups=mesh['ctx'=64,'head'=4] {'head'}, dimensions={0} | all-to-all | bytes 2097152 | tf_op jit(solution)/shard_map/cond/branch_0_fun/all_to_all | solution.py:699
  888.5 2.3 copy.230
  (1460 shorter events, 523.1 us)
Async XLA Ops:
  0.0 89.1 %copy-start.1 = (bf16[64,8192]{1,0:T(8,128)(2,1)S(1)}, bf16[64,8192]{1,0:T(8,128)(2,1)}, u32[]{:S(2)}) copy-start(bf16[64,8192]{1,0:T(8,128)(2,1)} %q_ref.1) | copy-start | bytes 3145732
  0.0 89.1 %copy-start.2 = (bf16[256,128]{1,0:T(8,128)(2,1)S(1)}, bf16[256,128]{1,0:T(8,128)(2,1)}, u32[]{:S(2)}) copy-start(bf16[256,128]{1,0:T(8,128)(2,1)} %k_ref.1) | copy-start | bytes 196612
  0.0 89.1 %copy-start.3 = (bf16[256,128]{1,0:T(8,128)(2,1)S(1)}, bf16[256,128]{1,0:T(8,128)(2,1)}, u32[]{:S(2)}) copy-start(bf16[256,128]{1,0:T(8,128)(2,1)} %v_ref.1) | copy-start | bytes 196612
  0.0 89.1 %copy-start.4 = (s32[8]{0:T(128)S(1)}, s32[8]{0:T(128)}, u32[]{:S(2)}) copy-start(s32[8]{0:T(128)} %len_ref.1) | copy-start | bytes 100
  224.8 100.7 %all-to-all-start.2 = ((bf16[64,256,128]{2,1,0:T(8,128)(2,1)}), bf16[64,256,128]{2,1,0:T(8,128)(2,1)}, u32[]{:S(2)}, u32[]{:S(2)}) async-start(bf16[64,256,128]{2,1,0:T(8,128)(2,1)} %tile.1), calls=%async_computation.2 | async-start | bytes 8388608 | tf_op jit(solution)/shard_map/cond/branch_0_fun/all_to_all | solution.py:663
  858.1 1.4 copy-start

commit v3 on v2

--- a/solution.py
+++ b/solution.py
@@ -220,7 +220,8 @@
         slot = my * 2 + mx
         remote(q_in.at[slot], q_in.at[slot], q_send.at[0], q_sem.at[slot], sibling).wait_recv()
 
-    z_start(0)
+    middle = (plane == 1) | (plane == 2)
+    pl.when(middle)(lambda: z_start(0))
     z_start(1)
     entry(0, 0, "start")
     for k in (1, 2, 3):
@@ -283,10 +284,17 @@
             pl.when(receiver)(lambda: sib_copy(pair, (xhi + side) % 2).start())
 
     near_half = same == 1
+
+    @pl.when(plane == 0)
+    def _():
+        z_copy(*z_hops[1][1:]).wait_send()
+        z_start(0)
+
     relay(0, 1, 4)
-    pl.when(near_half)(lambda: take_own(0))
+    pl.when(near_half & (yhi == 0))(lambda: take_own(0))
+    relay(1, 1, 2, 3)
+    pl.when(plane == 3)(lambda: z_start(0))
     relay(0, 2)
-    relay(1, 1, 2, 3)
     take_own(1)
 
     def norms(query_norm):
@@ -399,10 +407,9 @@
     def when_near(act, near):
         pl.when(same == near)(act)
 
-    far_steps = {('relay', 0): 1, ('relay', 2): 2, ('own', 0): 4, ('own', 2): 5, ('x', 1): 4, ('y', 1, 0): 7, ('y', 1, 1): 11, ('x', 0): 13, ('x', 2): 14, ('y', 0, 0): 18, ('y', 2, 0): 18}
-    near_steps = {('x', 0): 1, ('own', 2): 2, ('x', 1): 3, ('relay', 0): 4, ('relay', 2): 4, ('x', 2): 7, ('y', 1, 0): 7, ('y', 1, 1): 11, ('y', 0, 0): 18, ('y', 2, 0): 18}
-    last_keys = [('y', 0, 1), ('y', 2, 1)]
-    stat_steps = [6, 10, 15, 20]
+    far_steps = {('relay', 0): 1, ('relay', 2): 2, ('x', 1): 4, ('own', 'first'): 6, ('y', 1, 0): 7, ('own', 'second'): 9, ('x', 'first'): 10, ('y', 1, 1): 11, ('x', 'second'): 15, ('y', 'second', 0): 16}
+    near_steps = {('own', 'first'): 2, ('relay', 0): 2, ('relay', 2): 3, ('x', 1): 3, ('own', 'second'): 5, ('x', 'first'): 7, ('y', 1, 0): 7, ('y', 1, 1): 10, ('x', 'second'): 11, ('y', 'second', 0): 16}
+    stat_steps = [5, 8, 12, 15]
     events = []
     for key, at in far_steps.items():
         events.append((at, 0, key))
@@ -411,10 +418,15 @@
 
     def act_on(key):
         kind, back = key[0], key[1]
+        if back == "first":
+            back = 2 * yhi
+        elif back == "second":
+            back = 2 - 2 * yhi
         if kind == "relay":
             relay(1, back)
         elif kind == "own":
-            take_own(back)
+            early = (same == 1) & (yhi == 0) & (back == 0)
+            pl.when(jnp.logical_not(early))(lambda: take_own(back))
         elif kind == "x":
             take_x(back)
         else:
@@ -454,27 +466,23 @@
             before(step, at)
         chunk_step(step // 4, step % 4)
 
-    @pl.loop(16, 20)
+    def edge_step(slot):
+        last = quad_row - 7 * (1 - slot // 2)
+
+        @pl.when(last >= 0)
+        def _():
+            full_row(last, slot)
+
+        edge_rows(slot)
+
+    @pl.loop(16, 18)
     def _(step):
-        for at in range(16, 20):
+        for at in range(16, 18):
             before(step, at)
-        slot = slot_of(step - 16)
-        last = quad_row - 7 * (1 - slot // 2)
-
-        @pl.when(last >= 0)
-        def _():
-            full_row(last, slot)
-
-        edge_rows(slot)
-
-    @pl.loop(20, 24)
-    def _(step):
-        for at in range(20, 24):
-            before(step, at)
-        chunk_step(jnp.int32(4), step - 20)
-
-    for key in last_keys:
-        act_on(key)
+        edge_step(slot_of(19 - step))
+
+    act_on(("y", "second", 1))
+
     def o_columns():
         return pl.ds(pl.multiple_of(group * group_columns, 128), group_columns)
 
@@ -496,9 +504,15 @@
             o_part.at[own_slot], out_ref.at[:, columns], o_send.at[k], o_sem.at[k], sibling
         )
 
-    for k in (3, 2, 1, 0):
+    @pl.loop(0, 4)
+    def _(turn):
+        k = 3 - turn
         slot = slot_of(k)
-        chunk_step(jnp.int32(5), jnp.int32(k))
+        pl.when(turn >= 2)(lambda: edge_step(slot))
+
+        @pl.loop(4, 6)
+        def _(chunk):
+            chunk_step(chunk, k)
 
         for pair in range(8):
             columns = pl.ds(pl.multiple_of(slot * slot_columns + pair * 128, 128), 128)
@@ -506,8 +520,8 @@
             back = share.T.astype(jnp.bfloat16)
             o_part[slot, :, pl.ds(pair * 256, 128)] = back[:own_tokens]
             o_part[slot, :, pl.ds(pair * 256 + 128, 128)] = back[own_tokens:]
-        if k:
-            o_copy(k).start()
+        pl.when(k > 0)(lambda: o_copy(k).start())
+
     home = pltpu.make_async_copy(o_part.at[own_slot], out_ref.at[:, o_columns()], own_sem)
     home.start()
     stat_finish(3)
@@ -515,8 +529,9 @@
 
     for k in (1, 2, 3):
         q_copy(k).wait_send()
-    for hop in z_hops:
-        pl.when(hop[0])(lambda hop=hop: z_copy(*hop[1:]).wait_send())
+    for n, hop in enumerate(z_hops):
+        left = hop[0] & (plane > 0) if n == 1 else hop[0]
+        pl.when(left)(lambda hop=hop: z_copy(*hop[1:]).wait_send())
     for flip in range(2):
         for back in range(3):
             entry(flip, back, "wait")

time: 897 us -> 919 us (1.025)
  the two profiles are of different devices: /device:TPU:104 before, /device:TPU:100 now
where the time goes in v3:
time: 919 us; the launch traced here: 913 us
  matrix products  361 us (39%)
  blocking collectives  156 us (17%)
  other arithmetic  142 us (15%)
  waiting for transfers between devices  79.8 us (9%)
  Pallas kernels  77.8 us (8%)
  local copies, waits for them, and re-layouts  68 us (7%)
  loops' own time  18.2 us (2%)
    dot_general x136, matrix products, add_block(): jnp.dot(weights.astype(jnp.bfloat16), value_block, preferred_element_type...  192 us
    dot_general x136, matrix products, add_block(): lax.dot_general(tile_query, key_block, (((1,), (1,)), ((), ())), preferre...  169 us
    all_to_all x1, blocking collectives, from_all(): lax.all_to_all(copies, 'ctx', split_axis=0, concat_axis=0, tiled=True)  104 us
    add x140, other arithmetic, absorb(): positions = tile_start + jnp.arange(tok_rows, dtype=jnp.int32)  89.4 us
    all_to_all x1, waiting for transfers between devices, from_all(): lax.all_to_all(copies, 'ctx', split_axis=0, concat_axis=0, tiled=True)  79.8 us
    pallas_call x1, Pallas kernels, attend(): pl.pallas_call(attend_kernel, name='attend', out_shape=(jax.ShapeDtypeStr...  77.8 us
    reshape x136, local copies, waits for them, and re-layouts, add_block(): visible = jnp.repeat(visible, group_size, axis=0)  46.7 us
    reduce_sum x136, other arithmetic, add_block(): denominator = denominator * rescale + jnp.sum(weights, axis=1)  36.1 us
  transfers between devices with their start and end apart: 1, of which 1 were waited for; matrix products, arithmetic and copies ran while one was open for 1% of the time, Pallas kernels for 0%

profile of v3, /device:TPU:100, one launch (start us, length us, event | category | flops | bytes accessed | tf_op | source)
XLA Modules:
  0.0 912.7 jit_solution(14720728462492589711)
XLA Ops:
  0.0 77.8 %attend.1 = (bf16[64,8192]{1,0:T(8,128)(2,1)}, f32[1]{0:T(128)}) custom-call(bf16[64,8192]{1,0:T(8,128)(2,1)} %q_ref.1, bf16[256,128]{1,0:T(8,128)(2,1)} %k_ref.1, bf16[256,128]{1,0:T(8,128)(2,1)} %v_ref.1, s32[8]{0:T(128)} %len_ref.1), custom_call_target="tpu_custom_call" | custom-call | flops 19327352832 | bytes 4194304 | tf_op jit(solution)/shard_map/attend/pallas_call | solution.py:567
  78.5 831.9 %conditional.1 = (bf16[64,8192]{1,0:T(8,128)(2,1)}) conditional(s32[]{:T(128)} %bitcast.54, (s32[8]{0:T(128)S(1)}, bf16[256,128]{1,0:T(8,128)(2,1)S(1)}, bf16[256,128]{1,0:T(8,128)(2,1)S(1)}, bf16[64,8192]{1,0:T(8,128)(2,1)S(1)}) %tuple.245, bf16[64,8192]{1,0:T(8,128)(2,1)} %get-tuple-element.456), branch_computations={%region_0.42_spmd, %region_42.43_spmd} | conditional | flops 1095125504 | bytes 107736240 | solution.py:719
  78.7 27.1 %all_to_all.40 = bf16[64,4,2048]{2,0,1:T(8,128)(2,1)S(1)} all-to-all(bf16[64,4,2048]{2,0,1:T(8,128)(2,1)S(1)} %bitcast.161), channel_id=1, replica_groups=mesh['ctx'=64,'head'=4] {'head'}, dimensions={1} | all-to-all | bytes 2097152 | tf_op jit(solution)/shard_map/cond/branch_0_fun/all_to_all | solution.py:682
  106.8 104.4 %all_to_all.41 = bf16[64,256,128]{2,1,0:T(8,128)(2,1)} all-to-all(bf16[64,256,128]{2,1,0:T(8,128)(2,1)S(1)} %tile.0), channel_id=1, replica_groups=mesh['ctx'=64,'head'=4] {'ctx'}, dimensions={0} | all-to-all | bytes 8388608 | tf_op jit(solution)/shard_map/cond/branch_0_fun/all_to_all | solution.py:678
  211.3 3.0 tile.1
  214.2 8.8 all-to-all-start.2
  235.2 79.8 %all-to-all-done.2 = bf16[64,256,128]{2,1,0:T(8,128)(2,1)} async-done(((bf16[64,256,128]{2,1,0:T(8,128)(2,1)}), bf16[64,256,128]{2,1,0:T(8,128)(2,1)}, u32[]{:S(2)}, u32[]{:S(2)}) %all-to-all-start.2) | async-done | bytes 4194336 | tf_op jit(solution)/shard_map/cond/branch_0_fun/all_to_all | solution.py:678
  315.1 70.6 %while.113 = (s32[]{:T(128)}, f32[512]{0:T(512)S(1)}, f32[512]{0:T(512)S(1)}, f32[512,128]{1,0:T(8,128)S(1)}, s32[]{:T(128)}, /*index=5*/s32[32]{0:T(128)S(1)}, ...) while((s32[]{:T(128)}, f32[512]{0:T(512)S(1)}, ...), condition=%wide.region_11.11_spmd.clone, body=%wide.region_8.10_spmd.clone.sunk | while | flops 136758816 | bytes 5706307 | solution.py:664
  322.0 1.4 convolution_add_fusion.17
  385.7 71.9 %while.114 = (s32[]{:T(128)}, f32[512]{0:T(512)S(1)}, f32[512]{0:T(512)S(1)}, f32[512,128]{1,0:T(8,128)S(1)}, s32[]{:T(128)}, /*index=5*/s32[32]{0:T(128)S(1)}, ...) while((s32[]{:T(128)}, f32[512]{0:T(512)S(1)}, ...), condition=%wide.region_16.16_spmd.clone, body=%wide.region_13.15_spmd.clone.sunk | while | flops 136758816 | bytes 5706307 | solution.py:664
  392.8 1.4 convolution_add_fusion.18
  397.0 1.4 convolution_add_fusion.18
  405.5 1.4 convolution_add_fusion.18
  457.7 70.9 %while.115 = (s32[]{:T(128)}, f32[512]{0:T(512)S(1)}, f32[512]{0:T(512)S(1)}, f32[512,128]{1,0:T(8,128)S(1)}, s32[]{:T(128)}, /*index=5*/s32[32]{0:T(128)S(1)}, ...) while((s32[]{:T(128)}, f32[512]{0:T(512)S(1)}, ...), condition=%wide.region_21.21_spmd.clone, body=%wide.region_18.20_spmd.clone.sunk | while | flops 136758816 | bytes 5706307 | solution.py:664
  528.6 71.5 %while.116 = (s32[]{:T(128)}, f32[512]{0:T(512)S(1)}, f32[512]{0:T(512)S(1)}, f32[512,128]{1,0:T(8,128)S(1)}, s32[]{:T(128)}, /*index=5*/s32[32]{0:T(128)S(1)}, ...) while((s32[]{:T(128)}, f32[512]{0:T(512)S(1)}, ...), condition=%wide.region_26.26_spmd.clone, body=%wide.region_23.25_spmd.clone.sunk | while | flops 136758816 | bytes 5706307 | solution.py:664
  600.2 70.9 %while.117 = (s32[]{:T(128)}, f32[512]{0:T(512)S(1)}, f32[512]{0:T(512)S(1)}, f32[512,128]{1,0:T(8,128)S(1)}, s32[]{:T(128)}, /*index=5*/s32[32]{0:T(128)S(1)}, ...) while((s32[]{:T(128)}, f32[512]{0:T(512)S(1)}, ...), condition=%wide.region_31.31_spmd.clone, body=%wide.region_28.30_spmd.clone.sunk | while | flops 136758816 | bytes 5706307 | solution.py:664
  607.1 1.4 convolution_add_fusion.21
  671.1 69.6 %while.118 = (s32[]{:T(128)}, f32[512]{0:T(512)S(1)}, f32[512]{0:T(512)S(1)}, f32[512,128]{1,0:T(8,128)S(1)}, s32[]{:T(128)}, /*index=5*/s32[32]{0:T(128)S(1)}, ...) while((s32[]{:T(128)}, f32[512]{0:T(512)S(1)}, ...), condition=%wide.region_36.36_spmd.clone, body=%wide.region_33.35_spmd.clone.sunk | while | flops 136758816 | bytes 5706307 | solution.py:664
  677.9 1.4 convolution_add_fusion.22
  740.9 70.0 %while.119 = (s32[]{:T(128)}, f32[512]{0:T(512)S(1)}, f32[512]{0:T(512)S(1)}, f32[512,128]{1,0:T(8,128)S(1)}, s32[]{:T(128)}, /*index=5*/s32[32]{0:T(128)S(1)}, ...) while((s32[]{:T(128)}, f32[512]{0:T(512)S(1)}, ...), condition=%wide.region_41.41_spmd.clone, body=%wide.region_38.40_spmd.clone.sunk | while | flops 136758816 | bytes 5706307 | solution.py:664
  810.9 69.8 %while.112 = (s32[]{:T(128)}, f32[512]{0:T(512)S(1)}, f32[512]{0:T(512)S(1)}, f32[512,128]{1,0:T(8,128)S(1)}, s32[]{:T(128)}, /*index=5*/s32[32]{0:T(128)S(1)}, ...) while((s32[]{:T(128)}, f32[512]{0:T(512)S(1)}, ...), condition=%wide.region_6.6_spmd.clone, body=%wide.region_3.5_spmd.clone.sunk | while | flops 136758816 | bytes 5706307 | solution.py:664
  882.3 2.0 divide_convert_fusion
  884.8 24.6 %all_to_all.42 = bf16[4,64,2048]{2,1,0:T(8,128)(2,1)S(1)} all-to-all(bf16[4,64,2048]{2,1,0:T(8,128)(2,1)S(1)} %convert_element_type.35), channel_id=1, replica_groups=mesh['ctx'=64,'head'=4] {'head'}, dimensions={0} | all-to-all | bytes 2097152 | tf_op jit(solution)/shard_map/cond/branch_0_fun/all_to_all | solution.py:714
  910.5 2.3 copy.230
  (1548 shorter events, 555.6 us)
Async XLA Ops:
  0.0 78.5 %copy-start.1 = (bf16[64,8192]{1,0:T(8,128)(2,1)S(1)}, bf16[64,8192]{1,0:T(8,128)(2,1)}, u32[]{:S(2)}) copy-start(bf16[64,8192]{1,0:T(8,128)(2,1)} %q_ref.1) | copy-start | bytes 3145732
  0.0 78.5 %copy-start.2 = (bf16[256,128]{1,0:T(8,128)(2,1)S(1)}, bf16[256,128]{1,0:T(8,128)(2,1)}, u32[]{:S(2)}) copy-start(bf16[256,128]{1,0:T(8,128)(2,1)} %k_ref.1) | copy-start | bytes 196612
  0.0 78.5 %copy-start.3 = (bf16[256,128]{1,0:T(8,128)(2,1)S(1)}, bf16[256,128]{1,0:T(8,128)(2,1)}, u32[]{:S(2)}) copy-start(bf16[256,128]{1,0:T(8,128)(2,1)} %v_ref.1) | copy-start | bytes 196612
  0.0 78.5 %copy-start.4 = (s32[8]{0:T(128)S(1)}, s32[8]{0:T(128)}, u32[]{:S(2)}) copy-start(s32[8]{0:T(128)} %len_ref.1) | copy-start | bytes 100
  214.2 100.8 %all-to-all-start.2 = ((bf16[64,256,128]{2,1,0:T(8,128)(2,1)}), bf16[64,256,128]{2,1,0:T(8,128)(2,1)}, u32[]{:S(2)}, u32[]{:S(2)}) async-start(bf16[64,256,128]{2,1,0:T(8,128)(2,1)} %tile.1), calls=%async_computation.2 | async-start | bytes 8388608 | tf_op jit(solution)/shard_map/cond/branch_0_fun/all_to_all | solution.py:678
  880.9 1.4 copy-start

commit v4 on v3

--- a/solution.py
+++ b/solution.py
@@ -260,8 +260,12 @@
             @pl.when(receiver)
             def _():
                 x_copy(back).start()
-                pl.when(sent_on(back))(lambda: y_copy(back, 0).start())
                 sib_copy(pair, xhi).start()
+
+    def pass_own(back):
+        @pl.when((plane >= back) & receiver & sent_on(back))
+        def _():
+            y_copy(back, 0).start()
 
     def take_x(back):
         pair = (plane - back) * 2 + yhi
@@ -291,11 +295,19 @@
         z_start(0)
 
     relay(0, 1, 4)
-    pl.when(near_half & (yhi == 0))(lambda: take_own(0))
+    pl.when(plane == 3)(lambda: z_start(0))
+
+    @pl.when(near_half & (yhi == 0))
+    def _():
+        take_own(0)
+        pass_own(0)
+
     relay(1, 1, 2, 3)
-    pl.when(plane == 3)(lambda: z_start(0))
     relay(0, 2)
+    relay(1, 0)
+    relay(1, 2)
     take_own(1)
+    pass_own(1)
 
     def norms(query_norm):
         rank = lax.broadcasted_iota(jnp.int32, (8, 128), 0)
@@ -407,8 +419,8 @@
     def when_near(act, near):
         pl.when(same == near)(act)
 
-    far_steps = {('relay', 0): 1, ('relay', 2): 2, ('x', 1): 4, ('own', 'first'): 6, ('y', 1, 0): 7, ('own', 'second'): 9, ('x', 'first'): 10, ('y', 1, 1): 11, ('x', 'second'): 15, ('y', 'second', 0): 16}
-    near_steps = {('own', 'first'): 2, ('relay', 0): 2, ('relay', 2): 3, ('x', 1): 3, ('own', 'second'): 5, ('x', 'first'): 7, ('y', 1, 0): 7, ('y', 1, 1): 10, ('x', 'second'): 11, ('y', 'second', 0): 16}
+    far_steps = {('own', 'first'): 4, ('x', 1): 4, ('y', 1, 0): 7, ('own', 'second'): 8, ('pass', 'first'): 9, ('y', 1, 1): 11, ('x', 'first'): 12, ('x', 'second'): 15, ('y', 'second', 0): 17}
+    near_steps = {('own', 'first'): 2, ('pass', 'first'): 2, ('x', 1): 3, ('own', 'second'): 5, ('x', 'first'): 7, ('y', 1, 0): 7, ('y', 1, 1): 10, ('x', 'second'): 11, ('y', 'second', 0): 16}
     stat_steps = [5, 8, 12, 15]
     events = []
     for key, at in far_steps.items():
@@ -427,6 +439,9 @@
         elif kind == "own":
             early = (same == 1) & (yhi == 0) & (back == 0)
             pl.when(jnp.logical_not(early))(lambda: take_own(back))
+        elif kind == "pass":
+            early = (same == 1) & (yhi == 0) & (back == 0)
+            pl.when(jnp.logical_not(early))(lambda: pass_own(back))
         elif kind == "x":
             take_x(back)
         else:

time: 919 us -> 884 us (0.962)
  the two profiles are of different devices: /device:TPU:100 before, /device:TPU:98 now
where the time goes in v4:
time: 884 us; the launch traced here: 879 us
  matrix products  340 us (38%)
  blocking collectives  156 us (18%)
  other arithmetic  134 us (15%)
  waiting for transfers between devices  79.4 us (9%)
  Pallas kernels  78.2 us (9%)
  local copies, waits for them, and re-layouts  64.6 us (7%)
  loops' own time  17.5 us (2%)
  starting transfers between devices  8.94 us (1%)
    dot_general x128, matrix products, add_block(): jnp.dot(weights.astype(jnp.bfloat16), value_block, preferred_element_type...  181 us
    dot_general x128, matrix products, add_block(): lax.dot_general(tile_query, key_block, (((1,), (1,)), ((), ())), preferre...  159 us
    all_to_all x1, blocking collectives, from_all(): lax.all_to_all(copies, 'ctx', split_axis=0, concat_axis=0, tiled=True)  106 us
    add x132, other arithmetic, absorb(): positions = tile_start + jnp.arange(tok_rows, dtype=jnp.int32)  84.4 us
    all_to_all x1, waiting for transfers between devices, from_all(): lax.all_to_all(copies, 'ctx', split_axis=0, concat_axis=0, tiled=True)  79.4 us
    pallas_call x1, Pallas kernels, attend(): pl.pallas_call(attend_kernel, name='attend', out_shape=(jax.ShapeDtypeStr...  78.2 us
    reshape x128, local copies, waits for them, and re-layouts, add_block(): visible = jnp.repeat(visible, group_size, axis=0)  44 us
    reduce_sum x128, other arithmetic, add_block(): denominator = denominator * rescale + jnp.sum(weights, axis=1)  34 us
  transfers between devices with their start and end apart: 1, of which 1 were waited for; matrix products, arithmetic and copies ran while one was open for 1% of the time, Pallas kernels for 0%

profile of v4, /device:TPU:98, one launch (start us, length us, event | category | flops | bytes accessed | tf_op | source)
XLA Modules:
  0.0 879.1 jit_solution(7554728448587651164)
XLA Ops:
  0.0 78.2 %attend.1 = (bf16[64,8192]{1,0:T(8,128)(2,1)}, f32[1]{0:T(128)}) custom-call(bf16[64,8192]{1,0:T(8,128)(2,1)} %q_ref.1, bf16[256,128]{1,0:T(8,128)(2,1)} %k_ref.1, bf16[256,128]{1,0:T(8,128)(2,1)} %v_ref.1, s32[8]{0:T(128)} %len_ref.1), custom_call_target="tpu_custom_call" | custom-call | flops 19327352832 | bytes 4194304 | tf_op jit(solution)/shard_map/attend/pallas_call | solution.py:582
  79.0 797.9 %conditional.1 = (bf16[64,8192]{1,0:T(8,128)(2,1)}) conditional(s32[]{:T(128)} %bitcast.54, (s32[8]{0:T(128)S(1)}, bf16[256,128]{1,0:T(8,128)(2,1)S(1)}, bf16[256,128]{1,0:T(8,128)(2,1)S(1)}, bf16[64,8192]{1,0:T(8,128)(2,1)S(1)}) %tuple.245, bf16[64,8192]{1,0:T(8,128)(2,1)} %get-tuple-element.456), branch_computations={%region_0.42_spmd, %region_42.43_spmd} | conditional | flops 1095125504 | bytes 107736240 | solution.py:734
  79.1 28.6 %all_to_all.40 = bf16[64,4,2048]{2,0,1:T(8,128)(2,1)S(1)} all-to-all(bf16[64,4,2048]{2,0,1:T(8,128)(2,1)S(1)} %bitcast.161), channel_id=1, replica_groups=mesh['ctx'=64,'head'=4] {'head'}, dimensions={1} | all-to-all | bytes 2097152 | tf_op jit(solution)/shard_map/cond/branch_0_fun/all_to_all | solution.py:697
  108.7 106.2 %all_to_all.41 = bf16[64,256,128]{2,1,0:T(8,128)(2,1)} all-to-all(bf16[64,256,128]{2,1,0:T(8,128)(2,1)S(1)} %tile.0), channel_id=1, replica_groups=mesh['ctx'=64,'head'=4] {'ctx'}, dimensions={0} | all-to-all | bytes 8388608 | tf_op jit(solution)/shard_map/cond/branch_0_fun/all_to_all | solution.py:693
  214.9 3.0 tile.1
  217.9 8.9 %all-to-all-start.2 = ((bf16[64,256,128]{2,1,0:T(8,128)(2,1)}), bf16[64,256,128]{2,1,0:T(8,128)(2,1)}, u32[]{:S(2)}, u32[]{:S(2)}) async-start(bf16[64,256,128]{2,1,0:T(8,128)(2,1)} %tile.1), calls=%async_computation.2 | async-start | bytes 8388608 | tf_op jit(solution)/shard_map/cond/branch_0_fun/all_to_all | solution.py:693
  239.1 79.4 %all-to-all-done.2 = bf16[64,256,128]{2,1,0:T(8,128)(2,1)} async-done(((bf16[64,256,128]{2,1,0:T(8,128)(2,1)}), bf16[64,256,128]{2,1,0:T(8,128)(2,1)}, u32[]{:S(2)}, u32[]{:S(2)}) %all-to-all-start.2) | async-done | bytes 4194336 | tf_op jit(solution)/shard_map/cond/branch_0_fun/all_to_all | solution.py:693
  318.5 66.4 %while.113 = (s32[]{:T(128)}, f32[512]{0:T(512)S(1)}, f32[512]{0:T(512)S(1)}, f32[512,128]{1,0:T(8,128)S(1)}, s32[]{:T(128)}, /*index=5*/s32[32]{0:T(128)S(1)}, ...) while((s32[]{:T(128)}, f32[512]{0:T(512)S(1)}, ...), condition=%wide.region_11.11_spmd.clone, body=%wide.region_8.10_spmd.clone.sunk | while | flops 136758816 | bytes 5706307 | solution.py:679
  385.0 67.7 %while.114 = (s32[]{:T(128)}, f32[512]{0:T(512)S(1)}, f32[512]{0:T(512)S(1)}, f32[512,128]{1,0:T(8,128)S(1)}, s32[]{:T(128)}, /*index=5*/s32[32]{0:T(128)S(1)}, ...) while((s32[]{:T(128)}, f32[512]{0:T(512)S(1)}, ...), condition=%wide.region_16.16_spmd.clone, body=%wide.region_13.15_spmd.clone.sunk | while | flops 136758816 | bytes 5706307 | solution.py:679
  392.0 1.4 convolution_add_fusion.18
  452.7 66.7 %while.115 = (s32[]{:T(128)}, f32[512]{0:T(512)S(1)}, f32[512]{0:T(512)S(1)}, f32[512,128]{1,0:T(8,128)S(1)}, s32[]{:T(128)}, /*index=5*/s32[32]{0:T(128)S(1)}, ...) while((s32[]{:T(128)}, f32[512]{0:T(512)S(1)}, ...), condition=%wide.region_21.21_spmd.clone, body=%wide.region_18.20_spmd.clone.sunk | while | flops 136758816 | bytes 5706307 | solution.py:679
  519.5 67.3 %while.116 = (s32[]{:T(128)}, f32[512]{0:T(512)S(1)}, f32[512]{0:T(512)S(1)}, f32[512,128]{1,0:T(8,128)S(1)}, s32[]{:T(128)}, /*index=5*/s32[32]{0:T(128)S(1)}, ...) while((s32[]{:T(128)}, f32[512]{0:T(512)S(1)}, ...), condition=%wide.region_26.26_spmd.clone, body=%wide.region_23.25_spmd.clone.sunk | while | flops 136758816 | bytes 5706307 | solution.py:679
  586.8 66.7 %while.117 = (s32[]{:T(128)}, f32[512]{0:T(512)S(1)}, f32[512]{0:T(512)S(1)}, f32[512,128]{1,0:T(8,128)S(1)}, s32[]{:T(128)}, /*index=5*/s32[32]{0:T(128)S(1)}, ...) while((s32[]{:T(128)}, f32[512]{0:T(512)S(1)}, ...), condition=%wide.region_31.31_spmd.clone, body=%wide.region_28.30_spmd.clone.sunk | while | flops 136758816 | bytes 5706307 | solution.py:679
  597.9 1.4 convolution_add_fusion.21
  653.6 65.6 %while.118 = (s32[]{:T(128)}, f32[512]{0:T(512)S(1)}, f32[512]{0:T(512)S(1)}, f32[512,128]{1,0:T(8,128)S(1)}, s32[]{:T(128)}, /*index=5*/s32[32]{0:T(128)S(1)}, ...) while((s32[]{:T(128)}, f32[512]{0:T(512)S(1)}, ...), condition=%wide.region_36.36_spmd.clone, body=%wide.region_33.35_spmd.clone.sunk | while | flops 136758816 | bytes 5706307 | solution.py:679
  660.4 1.4 convolution_add_fusion.22
  719.2 65.7 %while.119 = (s32[]{:T(128)}, f32[512]{0:T(512)S(1)}, f32[512]{0:T(512)S(1)}, f32[512,128]{1,0:T(8,128)S(1)}, s32[]{:T(128)}, /*index=5*/s32[32]{0:T(128)S(1)}, ...) while((s32[]{:T(128)}, f32[512]{0:T(512)S(1)}, ...), condition=%wide.region_41.41_spmd.clone, body=%wide.region_38.40_spmd.clone.sunk | while | flops 136758816 | bytes 5706307 | solution.py:679
  746.5 1.4 convolution_add_fusion.23
  771.2 1.4 convolution_add_fusion.23
  785.0 65.9 %while.112 = (s32[]{:T(128)}, f32[512]{0:T(512)S(1)}, f32[512]{0:T(512)S(1)}, f32[512,128]{1,0:T(8,128)S(1)}, s32[]{:T(128)}, /*index=5*/s32[32]{0:T(128)S(1)}, ...) while((s32[]{:T(128)}, f32[512]{0:T(512)S(1)}, ...), condition=%wide.region_6.6_spmd.clone, body=%wide.region_3.5_spmd.clone.sunk | while | flops 136758816 | bytes 5706307 | solution.py:679
  792.0 1.4 convolution_add_fusion.16
  852.5 2.0 divide_convert_fusion
  855.0 20.8 %all_to_all.42 = bf16[4,64,2048]{2,1,0:T(8,128)(2,1)S(1)} all-to-all(bf16[4,64,2048]{2,1,0:T(8,128)(2,1)S(1)} %convert_element_type.35), channel_id=1, replica_groups=mesh['ctx'=64,'head'=4] {'head'}, dimensions={0} | all-to-all | bytes 2097152 | tf_op jit(solution)/shard_map/cond/branch_0_fun/all_to_all | solution.py:729
  876.9 2.3 copy.230
  (1460 shorter events, 523.1 us)
Async XLA Ops:
  0.0 78.9 %copy-start.1 = (bf16[64,8192]{1,0:T(8,128)(2,1)S(1)}, bf16[64,8192]{1,0:T(8,128)(2,1)}, u32[]{:S(2)}) copy-start(bf16[64,8192]{1,0:T(8,128)(2,1)} %q_ref.1) | copy-start | bytes 3145732
  0.0 78.9 %copy-start.2 = (bf16[256,128]{1,0:T(8,128)(2,1)S(1)}, bf16[256,128]{1,0:T(8,128)(2,1)}, u32[]{:S(2)}) copy-start(bf16[256,128]{1,0:T(8,128)(2,1)} %k_ref.1) | copy-start | bytes 196612
  0.0 78.9 %copy-start.3 = (bf16[256,128]{1,0:T(8,128)(2,1)S(1)}, bf16[256,128]{1,0:T(8,128)(2,1)}, u32[]{:S(2)}) copy-start(bf16[256,128]{1,0:T(8,128)(2,1)} %v_ref.1) | copy-start | bytes 196612
  0.0 78.9 %copy-start.4 = (s32[8]{0:T(128)S(1)}, s32[8]{0:T(128)}, u32[]{:S(2)}) copy-start(s32[8]{0:T(128)} %len_ref.1) | copy-start | bytes 100
  217.9 100.6 %all-to-all-start.2 = ((bf16[64,256,128]{2,1,0:T(8,128)(2,1)}), bf16[64,256,128]{2,1,0:T(8,128)(2,1)}, u32[]{:S(2)}, u32[]{:S(2)}) async-start(bf16[64,256,128]{2,1,0:T(8,128)(2,1)} %tile.1), calls=%async_computation.2 | async-start | bytes 8388608 | tf_op jit(solution)/shard_map/cond/branch_0_fun/all_to_all | solution.py:693
  851.1 1.4 copy-start
